TPU v7x, 256 devices: a whole 4x4x8 slice. The times are simulated.
256 devices in a mesh: fibre: 8 (over y, core), record: 32 (over x, z).
Axes of the slice: x: 4, y: 4, z: 8, core: 2. Of those that a mesh axis runs over, the one named last changes fastest.
Arguments:
- records: bfloat16 [32, 64, 64, 1024], P('record', 'fibre'), may hold values from -80 to 80, as said below
- labels: int32 [32, 64, 1024], P('record', 'fibre'), may hold values from 0 to 1
- w_time: bfloat16 [7, 64, 64], replicated, may hold values from -0.25 to 0.25
- b_time: float32 [64], replicated, may hold values from -3 to 3
- w_fibre: bfloat16 [7, 64, 64], replicated, may hold values from -0.25 to 0.25
- gamma: float32 [64], replicated, may hold values from 0.1 to 1.9
- beta: float32 [64], replicated, may hold values from -3 to 3
- w_head: bfloat16 [64], replicated, may hold values from -0.75 to 0.75
- b_head: float32 [1], replicated, may hold values from -3 to 3
Outputs:
- grad_records: bfloat16 [32, 64, 64, 1024], P('record', 'fibre')
- grad_w_time: float32 [7, 64, 64], replicated
- grad_b_time: float32 [64], replicated
- grad_w_fibre: float32 [7, 64, 64], replicated
- grad_gamma: float32 [64], replicated
- grad_beta: float32 [64], replicated
- grad_w_head: float32 [64], replicated
- loss: float32 [], replicated
Inputs may be any that keep to these rules, and one draw needn't show every extreme that they name: `records`: field samples.
All inputs are finite; a program needn't handle non-finite values.
Results may differ from a plain program's by a relative error of at most 0.0081.
Values may be sent and summed in bfloat16 or wider, within the bound.
A program may use at most 64 MiB of HBM per device.

v0:
```python
import jax
import jax.numpy as jnp
from jax import lax
from jax.sharding import PartitionSpec as P

TEMPORAL_TAPS = 7
TIME_DILATION = 2
KC = 7


EPS = 1e-05


def silu_slope(value):
    sig = jax.nn.sigmoid(value)
    return sig * (1.0 + value * (1.0 - sig))


def time_taps(strain_field, weights):
    window_size = strain_field.shape[3]
    halfwidth = (weights.shape[0] - 1) // 2
    padded_input = jnp.pad(
        strain_field,
        ((0, 0), (0, 0), (0, 0), (TIME_DILATION * halfwidth, TIME_DILATION * halfwidth)),
    )
    grand_total = jnp.zeros(
        (strain_field.shape[0], strain_field.shape[1], weights.shape[1], window_size), jnp.float32
    )
    for tap_index in range(weights.shape[0]):
        grand_total = grand_total + jnp.einsum(
            "gf,rcfs->rcgs",
            weights[tap_index],
            padded_input[
                :, :, :, TIME_DILATION * tap_index : TIME_DILATION * tap_index + window_size
            ],
            preferred_element_type=jnp.float32,
        )
    return grand_total


def fibre_taps(padded_input, weights, count):
    grand_total = jnp.zeros(
        (padded_input.shape[0], count, weights.shape[1], padded_input.shape[3]), jnp.float32
    )
    for tap_index in range(weights.shape[0]):
        grand_total = grand_total + jnp.einsum(
            "gf,rcfs->rcgs",
            weights[tap_index],
            padded_input[:, tap_index : tap_index + count],
            preferred_element_type=jnp.float32,
        )
    return grand_total


def local(records, labels, w_time, b_time, w_fibre, gamma, beta, w_head, b_head):
    temporal_halfwidth = (TEMPORAL_TAPS - 1) // 2
    half_c = (KC - 1) // 2
    cells = records.shape[1] * records.shape[3] * lax.axis_size("fibre")
    cell_count_total = float(cells * records.shape[0] * lax.axis_size("record"))
    cells = float(cells)
    pre = time_taps(records, w_time) + b_time[None, None, :, None]
    hidden = jax.nn.silu(pre).astype(jnp.bfloat16)
    working = lax.all_to_all(hidden, "fibre", split_axis=3, concat_axis=1, tiled=True)
    count = working.shape[1]
    hidden_pad = jnp.pad(working, ((0, 0), (half_c, half_c), (0, 0), (0, 0)))
    second_preactivation = fibre_taps(hidden_pad, w_fibre, count)
    first = lax.psum(jnp.sum(second_preactivation, axis=(0, 1, 3)), ("fibre", "record"))
    channel_mean = first / cell_count_total
    centered = second_preactivation - channel_mean[None, None, :, None]
    second = lax.psum(jnp.sum(centered * centered, axis=(0, 1, 3)), ("fibre", "record"))
    var = second / cell_count_total
    inverse_deviation = lax.rsqrt(var + EPS)
    normalized_input = (
        second_preactivation - channel_mean[None, None, :, None]
    ) * inverse_deviation[None, None, :, None]
    activation = gamma[None, None, :, None] * normalized_input + beta[None, None, :, None]
    normed = jax.nn.silu(activation).astype(jnp.bfloat16)
    normed_head = lax.all_to_all(normed, "fibre", split_axis=1, concat_axis=3, tiled=True)
    logit = (
        jnp.einsum("rcfs,f->rcs", normed_head, w_head, preferred_element_type=jnp.float32)
        + b_head[0]
    )
    target = labels.astype(jnp.float32)
    partial_loss = jnp.sum(jnp.log1p(jnp.exp(logit)) - target * logit)
    loss_total = lax.psum(partial_loss, ("fibre", "record"))
    dlogit = jax.nn.sigmoid(logit) - target
    head_output_gradient = jnp.einsum("rcs,rcfs->f", dlogit, normed_head.astype(jnp.float32))
    dnormed = (dlogit[:, :, None, :] * w_head.astype(jnp.float32)[None, None, :, None]).astype(
        jnp.bfloat16
    )
    dnormed_work = lax.all_to_all(dnormed, "fibre", split_axis=3, concat_axis=1, tiled=True)
    activation_gradient = dnormed_work.astype(jnp.float32) * silu_slope(activation)
    beta_total_sum, gamma_total_sum = lax.psum(
        (
            jnp.sum(activation_gradient, axis=(0, 1, 3)),
            jnp.sum(activation_gradient * normalized_input, axis=(0, 1, 3)),
        ),
        ("fibre", "record"),
    )
    scale_g = (gamma * inverse_deviation)[None, None, :, None]
    second_preact_gradient = (
        scale_g
        * (
            activation_gradient
            - beta_total_sum[None, None, :, None] / cell_count_total
            - normalized_input * gamma_total_sum[None, None, :, None] / cell_count_total
        )
    ).astype(jnp.bfloat16)
    fibre_grad = jnp.stack(
        [
            jnp.einsum(
                "rcgs,rcfs->gf",
                second_preact_gradient,
                hidden_pad[:, tap_index : tap_index + count],
                preferred_element_type=jnp.float32,
            )
            for tap_index in range(KC)
        ]
    )
    dz2_pad = jnp.pad(second_preact_gradient, ((0, 0), (half_c, half_c), (0, 0), (0, 0)))
    dhidden = jnp.zeros(
        (second_preact_gradient.shape[0], count, w_fibre.shape[2], second_preact_gradient.shape[3]),
        jnp.float32,
    )
    for tap_index in range(KC):
        dhidden = dhidden + jnp.einsum(
            "gf,rcgs->rcfs",
            w_fibre[tap_index],
            dz2_pad[:, 2 * half_c - tap_index : 2 * half_c - tap_index + count],
            preferred_element_type=jnp.float32,
        )
    dhidden = dhidden.astype(jnp.bfloat16)
    dhidden = lax.all_to_all(dhidden, "fibre", split_axis=1, concat_axis=3, tiled=True)
    dz1 = (dhidden.astype(jnp.float32) * silu_slope(pre)).astype(jnp.bfloat16)
    bias_grad = jnp.sum(dz1.astype(jnp.float32), axis=(0, 1, 3))
    window_size = records.shape[3]
    padding_amount = TIME_DILATION * temporal_halfwidth
    padded_records = jnp.pad(records, ((0, 0), (0, 0), (0, 0), (padding_amount, padding_amount)))
    dz1_pad = jnp.pad(dz1, ((0, 0), (0, 0), (0, 0), (padding_amount, padding_amount)))
    temporal_gradient = jnp.stack(
        [
            jnp.einsum(
                "rcgs,rcfs->gf",
                dz1,
                padded_records[
                    :, :, :, TIME_DILATION * tap_index : TIME_DILATION * tap_index + window_size
                ],
                preferred_element_type=jnp.float32,
            )
            for tap_index in range(TEMPORAL_TAPS)
        ]
    )
    back = jnp.zeros(records.shape, jnp.float32)
    for tap_index in range(TEMPORAL_TAPS):
        window_start = TIME_DILATION * (2 * temporal_halfwidth - tap_index)
        back = back + jnp.einsum(
            "gf,rcgs->rcfs",
            w_time[tap_index],
            dz1_pad[:, :, :, window_start : window_start + window_size],
            preferred_element_type=jnp.float32,
        )
    grad_records = back.astype(jnp.bfloat16)
    local_terms = (
        temporal_gradient / cells,
        bias_grad / cells,
        fibre_grad / cells,
        head_output_gradient / cells,
    )
    grad_w_time, grad_b_time, grad_w_fibre, grad_w_head = lax.psum(
        (local_terms[0], local_terms[1], local_terms[2], local_terms[3]), ("fibre", "record")
    )
    loss = loss_total / cell_count_total
    return (
        grad_records,
        grad_w_time,
        grad_b_time,
        grad_w_fibre,
        gamma_total_sum / cells,
        beta_total_sum / cells,
        grad_w_head,
        loss,
    )


def solution(mesh):
    return jax.shard_map(
        local,
        mesh=mesh,
        in_specs=(
            P("record", "fibre", None, None),
            P("record", "fibre", None),
            P(),
            P(),
            P(),
            P(),
            P(),
            P(),
            P(),
        ),
        out_specs=(P("record", "fibre", None, None), P(), P(), P(), P(), P(), P(), P()),
        check_vma=False,
    )
```

profile of v0, /device:TPU:1, one launch (start us, length us, event | category | flops | bytes accessed | tf_op | source)
XLA Modules:
  0.0 660.6 jit_solution(6548120653741548095)
XLA Ops:
  7.2 1.8 fusion.104
  11.7 2.6 fusion.9
  14.3 2.5 copy.99
  16.8 3.4 reshape.349
  20.2 20.8 %all_to_all.51 = bf16[8,2,32768]{2,1,0:T(2,128)(2,1)S(1)} all-to-all(bf16[8,2,32768]{2,1,0:T(2,128)(2,1)S(1)} %reshape.349), channel_id=1, replica_groups=mesh['fibre'=8,'record'=32] {'fibre'}, dimensions={0} | all-to-all | bytes 2097152 | tf_op jit(solution)/shard_map/all_to_all | solution.py:63
  41.0 2.7 reshape.350
  43.7 2.3 copy.100
  48.5 2.3 fusion.285
  50.8 78.8 %psum.63 = f32[64]{0:T(128)S(1)} all-reduce(f32[64]{0:T(128)S(1)} %get-tuple-element.28), channel_id=1, replica_groups=mesh['fibre'=8,'record'=32] {'fibre','record'}, use_global_device_ids=true, to_apply=%region_1.2 | all-reduce | flops 64 | bytes 512 | tf_op jit(solution)/shard_map/psum | solution.py:67
  129.6 2.0 multiply_reduce_fusion
  131.6 73.1 %psum.64 = f32[64]{0:T(128)S(1)} all-reduce(f32[64]{0:T(128)S(1)} %multiply_reduce_fusion), channel_id=1, replica_groups=mesh['fibre'=8,'record'=32] {'fibre','record'}, use_global_device_ids=true, to_apply=%region_3.4 | all-reduce | flops 64 | bytes 512 | tf_op jit(solution)/shard_map/psum | solution.py:70
  204.7 3.3 fusion.121
  208.1 4.4 all-to-all-start.1
  213.2 14.4 %all-to-all-done.1 = bf16[1,64,64,128]{3,2,0,1:T(8,128)(2,1)S(1)} async-done(((bf16[1,64,64,128]{3,2,0,1:T(8,128)(2,1)}), bf16[1,64,64,128]{3,2,0,1:T(8,128)(2,1)S(1)}, u32[]{:S(2)}, u32[]{:S(2)}) %all-to-all-start.1) | async-done | bytes 1048608 | tf_op jit(solution)/shard_map/all_to_all | solution.py:78
  227.6 1.7 copy.167
  229.3 1.5 reshape.270
  232.7 3.2 fusion.286
  235.9 4.3 reshape.351
  240.3 4.3 all-to-all-start.2
  244.6 1.6 fusion.31
  246.2 13.5 %all-to-all-done.2 = bf16[8,2,32768]{2,1,0:T(2,128)(2,1)S(1)} async-done(((bf16[8,2,32768]{2,1,0:T(2,128)(2,1)}), bf16[8,2,32768]{2,1,0:T(2,128)(2,1)S(1)}, u32[]{:S(2)}, u32[]{:S(2)}) %all-to-all-start.2) | async-done | bytes 1048608 | tf_op jit(solution)/shard_map/all_to_all | solution.py:91
  259.7 2.7 reshape.352
  262.4 2.5 copy.104
  265.6 1.2 copy-done.1
  266.8 2.6 fusion.283
  269.4 74.5 %all-reduce.5 = (f32[64]{0:T(128)S(1)}, f32[64]{0:T(128)S(1)}) all-reduce(f32[64]{0:T(128)S(1)} %get-tuple-element.9, f32[64]{0:T(128)S(1)} %get-tuple-element.8), channel_id=1, replica_groups=mesh['fibre'=8,'record'=32] {'fibre','record'}, use_global_device_ids=true, to_apply=%region_7.8 | all-reduce | flops 128 | bytes 1024 | tf_op jit(solution)/shard_map/psum | solution.py:93
  344.4 2.9 fusion.5
  352.2 1.0 fusion.21
  355.3 1.9 fusion.15
  357.2 4.8 all-to-all-start.3
  362.5 1.0 fusion.18
  363.6 1.0 fusion.17
  364.6 1.6 broadcast_multiply_fusion
  366.2 11.0 %all-to-all-done.3 = bf16[1,64,64,128]{3,2,0,1:T(8,128)(2,1)} async-done(((bf16[1,64,64,128]{3,2,0,1:T(8,128)(2,1)}), bf16[1,64,64,128]{3,2,0,1:T(8,128)(2,1)}, u32[]{:S(2)}, u32[]{:S(2)}) %all-to-all-start.3) | async-done | bytes 1048608 | tf_op jit(solution)/shard_map/all_to_all | solution.py:133
  377.2 3.1 copy.166
  380.4 2.7 reshape.289
  383.1 3.1 convert_reduce_fusion
  386.8 2.0 fusion.46
  388.8 2.0 fusion.35
  390.7 2.0 fusion.33
  392.7 1.9 fusion.48
  394.7 1.8 fusion.44
  396.5 2.0 fusion.50
  402.6 7.3 %fusion.16 = bf16[1,8,64,1024]{3,2,1,0:T(8,128)(2,1)} fusion(f32[8,1024,64]{1,2,0:T(8,128)} %fusion.33, f32[8,1024,64]{1,2,0:T(8,128)} %fusion.35, f32[8,1024,64]{1,2,0:T(8,128)} %fusion.44, f32[8,1024,64]{1,2,0:T(8,128)} %fusion.46, f32[8,1024,64]{1,2,0:T(8,128)} %fusion.50, f32[8,1024,64]{1,2,0:T(8,128)} %fusion.48, ...), kind=kOutput, calls=%fused_computation.34 | convolution fusion | flops 70778880 | bytes 14696448 | tf_op jit(solution)/shard_map/gf,rcgs->rcfs/dot_general | solution.py:156
  409.9 74.3 %all-reduce.4 = (f32[64]{0:T(128)}, f32[64]{0:T(128)}, f32[]{:T(128)}) all-reduce(f32[64]{0:T(128)S(1)} %broadcast_multiply_fusion.4, f32[64]{0:T(128)S(1)} %fusion.31, f32[]{:T(128)} %get-tuple-element.20), channel_id=1, replica_groups=mesh['fibre'=8,'record'=32] {'fibre','record'}, use_global_device_ids=true, to_apply=%region_10.11 | all-reduce | flops 129 | bytes 1032 | tf_op jit(solution)/shard_map/psum | solution.py:169
  484.9 164.4 %all-reduce.9.cloned.1.call-done = (f32[7,64,64]{2,1,0:T(8,128)}, f32[7,64,64]{2,1,0:T(8,128)}) async-done(((f32[7,64,64]{2,1,0:T(8,128)}, f32[7,64,64]{2,1,0:T(8,128)}), (f32[7,64,64]{2,1,0:T(8,128)}, f32[7,64,64]{2,1,0:T(8,128)})) %all-reduce.9.cloned.1.call-update) | async-done | bytes 229392 | tf_op jit(solution)/shard_map/psum | solution.py:169
  649.3 1.6 copy.183
  651.0 1.6 copy.184
  (62 shorter events, 20.2 us)
Async XLA Ops:
  7.2 1.9 copy-start.4
  7.2 1.9 copy-start
  11.0 0.7 copy-start.8
  43.7 2.3 copy-start.3
  50.8 153.9 %copy-start.6 = (f32[64]{0:T(128)S(1)}, f32[64]{0:T(128)}, u32[]{:S(2)}) copy-start(f32[64]{0:T(128)} %param.14) | copy-start | bytes 772
  50.8 153.9 %copy-start.7 = (f32[64]{0:T(128)S(1)}, f32[64]{0:T(128)}, u32[]{:S(2)}) copy-start(f32[64]{0:T(128)} %param.15) | copy-start | bytes 772
  204.7 8.4 %copy-start.9 = (bf16[64]{0:T(256)(128)(2,1)S(1)}, bf16[64]{0:T(256)(128)(2,1)}, u32[]{:S(2)}) copy-start(bf16[64]{0:T(256)(128)(2,1)} %param.16) | copy-start | bytes 388
  208.1 19.5 %all-to-all-start.1 = ((bf16[1,64,64,128]{3,2,0,1:T(8,128)(2,1)}), bf16[1,64,64,128]{3,2,0,1:T(8,128)(2,1)S(1)}, u32[]{:S(2)}, u32[]{:S(2)}) async-start(bf16[1,64,64,128]{3,2,0,1:T(8,128)(2,1)} %fusion.121), calls=%async_computation.1 | async-start | bytes 2097152 | tf_op jit(solution)/shard_map/all_to_all | solution.py:78
  229.3 1.8 copy-start.5
  230.8 5.1 copy-start.2
  240.3 19.5 %all-to-all-start.2 = ((bf16[8,2,32768]{2,1,0:T(2,128)(2,1)}), bf16[8,2,32768]{2,1,0:T(2,128)(2,1)S(1)}, u32[]{:S(2)}, u32[]{:S(2)}) async-start(bf16[8,2,32768]{2,1,0:T(2,128)(2,1)} %reshape.351), calls=%async_computation.2 | async-start | bytes 2097152 | tf_op jit(solution)/shard_map/all_to_all | solution.py:91
  265.2 1.6 copy-start.1
  357.2 20.0 %all-to-all-start.3 = ((bf16[1,64,64,128]{3,2,0,1:T(8,128)(2,1)}), bf16[1,64,64,128]{3,2,0,1:T(8,128)(2,1)}, u32[]{:S(2)}, u32[]{:S(2)}) async-start(bf16[1,64,64,128]{3,2,0,1:T(8,128)(2,1)} %fusion.15), calls=%async_computation.3 | async-start | bytes 2097152 | tf_op jit(solution)/shard_map/all_to_all | solution.py:133
  362.0 287.3 %all-reduce.9.cloned.1.call-start = ((), (), s32[]{:S(2)}) async-start(), calls=%async_computation.4 | async-start | bytes 917504 | tf_op jit(solution)/shard_map/psum | solution.py:169
Sparse Core Ops, SparseCore 0:
  402.7 246.5 all-reduce.8
where the time goes:
time: 662 us; the launch traced here: 661 us
  blocking collectives  322 us (49%)
  waiting for transfers between devices  203 us (31%)
  matrix products  48.5 us (7%)
  local copies, waits for them, and re-layouts  35.8 us (5%)
  other arithmetic  21.1 us (3%)
  between operations  16.8 us (3%)
  starting transfers between devices  13.5 us (2%)
    psum x1, waiting for transfers between devices, local(): lax.psum((local_terms[0], local_terms[1], local_terms[2], local_terms[3])...  164 us
    psum x1, blocking collectives, local(): lax.psum(jnp.sum(second_preactivation, axis=(0, 1, 3)), ('fibre', 'record'))  78.8 us
    psum x1, blocking collectives, local(): lax.psum((jnp.sum(activation_gradient, axis=(0, 1, 3)), jnp.sum(activatio...  74.5 us
    psum x1, blocking collectives, local(): lax.psum((local_terms[0], local_terms[1], local_terms[2], local_terms[3])...  74.3 us
    psum x1, blocking collectives, local(): lax.psum(jnp.sum(centered * centered, axis=(0, 1, 3)), ('fibre', 'record'))  73.1 us
    all_to_all x1, blocking collectives, local(): lax.all_to_all(hidden, 'fibre', split_axis=3, concat_axis=1, tiled=True)  20.8 us
    dot_general x7, matrix products, local(): jnp.einsum('gf,rcgs->rcfs', w_time[tap_index], dz1_pad[:, :, :, window_st...  19.1 us
    unnamed x27, local copies, waits for them, and re-layouts  18 us
  transfers between devices with their start and end apart: 4, of which 4 were waited for; matrix products, arithmetic and copies ran while one was open for 2% of the time, Pallas kernels for 0%

commit v1 on v0

v1 whole, which is shorter than its diff:
```python
import functools

import jax
import jax.numpy as jnp
from jax import lax
from jax.experimental import pallas as pl
from jax.experimental.pallas import tpu as pltpu
from jax.sharding import PartitionSpec as P

F = 64
TAPS = 7
DILATION = 2
HALF = 3
EPS = 1e-05
BF = jnp.bfloat16
F32 = jnp.float32
MESH = pl.DeviceIdType.MESH
NT = (((1,), (1,)), ((), ()))


def mm(a, b):
    return jnp.dot(a, b, preferred_element_type=F32)


def sigmoid(v):
    return 1.0 / (1.0 + jnp.exp(-v))


def eye():
    return lax.broadcasted_iota(jnp.int32, (F, F), 0) == lax.broadcasted_iota(jnp.int32, (F, F), 1)


def to_col(row):
    return jnp.sum(jnp.where(eye(), jnp.broadcast_to(row, (F, F)), 0.0), axis=1, keepdims=True)


def to_row(col):
    return jnp.sum(jnp.where(eye(), jnp.broadcast_to(col, (F, F)), 0.0), axis=0, keepdims=True)


def wide(row):
    return jnp.broadcast_to(to_col(row), (F, 128))


class Group:
    def __init__(self, n, me, target, send, recv):
        self.n, self.me, self.target, self.send, self.recv = n, me, target, send, recv

    def peers(self):
        return [lax.rem(self.me + d, self.n) for d in range(1, self.n)]

    def copy(self, src, dst, p, slot):
        return pltpu.make_async_remote_copy(
            src_ref=src,
            dst_ref=dst,
            send_sem=self.send.at[p],
            recv_sem=self.recv.at[slot],
            device_id=self.target(p),
            device_id_type=MESH,
        )

    def spread(self, buf):
        for p in self.peers():
            self.copy(buf.at[self.me], buf.at[self.me], p, self.me).start()

    def scatter(self, src, buf):
        for p in self.peers():
            self.copy(src.at[p], buf.at[self.me], p, self.me).start()

    def arrive(self, buf):
        for p in self.peers():
            self.copy(buf.at[p], buf.at[p], p, p).wait_recv()

    def done(self, buf):
        for p in self.peers():
            self.copy(buf.at[p], buf.at[p], p, p).wait_send()


def kernel(
    dims,
    x_ref, lab_ref, wt_ref, bt_ref, wf_ref, gam_ref, bet_ref, wh_ref, bh_ref,
    gr_ref, gwt_ref, gbt_ref, gwf_ref, gga_ref, gbe_ref, gwh_ref, loss_ref,
    wts, wtt, wfb, wfr, xcol, dcol, h1, sl1, z2, sl2, dz2, dz1, par, acc, accr, lab, dl, dll, dlr,
    gt,
    sf1, sx1, sz1, sf2, sx2, sz2,
    ga, ra, xa, za, fa, gb, rb, xb, zb, fb,
    hs, hr, ds, dr,
    f1s, f1r, x1s, x1r, z1s, z1r, f2s, f2r, x2s, x2r, z2s, z2r,
    a1s, a1r, a2s, a2r, a3s, a3r, a4s, a4r,
    b1s, b1r, b2s, b2r, b3s, b3r, b4s, b4r,
):
    nf, nx, nz, C, T = dims
    total = float(nf * nx * nz * C * T)
    cells = float(nf * C * T)
    fi = lax.axis_index("fibre")
    ri = lax.axis_index("record")
    xi, zi = ri // nz, lax.rem(ri, nz)

    def to_f(p):
        return (p, ri)

    def to_x(p):
        return (fi, p * nz + zi)

    def to_z(p):
        return (fi, xi * nz + p)

    def group_f(s, r):
        return Group(nf, fi, to_f, s, r)

    def group_x(s, r):
        return Group(nx, xi, to_x, s, r)

    def group_z(s, r):
        return Group(nz, zi, to_z, s, r)

    barrier = pltpu.get_barrier_semaphore()
    for group in (group_f(None, None), group_x(None, None), group_z(None, None)):
        for p in group.peers():
            pl.semaphore_signal(barrier, inc=1, device_id=group.target(p), device_id_type=MESH)

    for k in range(TAPS):
        wts[:, k * F:(k + 1) * F] = wt_ref[k]
        wtt[:, k * F:(k + 1) * F] = wt_ref[k].astype(F32).T.astype(BF)
    wfb[...] = jnp.zeros_like(wfb)
    wfr[...] = jnp.zeros_like(wfr)
    for k in range(TAPS):
        w = wf_ref[k]
        wr = wf_ref[TAPS - 1 - k].astype(F32).T.astype(BF)
        for j in range(4):
            wfb[j * F:(j + 1) * F, (j + k) * F:(j + k + 1) * F] = w
            wfr[j * F:(j + 1) * F, (j + k) * F:(j + k + 1) * F] = wr
    for c in range(C):
        lab[c] = lab_ref[c:c + 1, :].astype(F32)
    par[0] = wide(bt_ref[...])
    acc[...] = jnp.zeros_like(acc)
    accr[...] = jnp.zeros_like(accr)

    pl.semaphore_wait(barrier, nf + nx + nz - 3)

    has_l, has_r = fi > 0, fi < nf - 1
    left, right = lax.rem(fi + nf - 1, nf), lax.rem(fi + 1, nf)

    @pl.when(jnp.logical_not(has_l))
    def _():
        for i in range(2 * HALF):
            h1[i] = jnp.zeros((F, T), BF)
        for i in range(HALF):
            dz2[i] = jnp.zeros((F, T), BF)

    @pl.when(jnp.logical_not(has_r))
    def _():
        for i in range(2 * HALF):
            h1[2 * HALF + C + i] = jnp.zeros((F, T), BF)
        for i in range(HALF):
            dz2[HALF + C + i] = jnp.zeros((F, T), BF)

    def halo(c, side):
        slot = c + 2 * HALF + C if side == "l" else c + 2 * HALF - C
        index = c + 2 * HALF if side == "l" else c + 2 * HALF - C
        return pltpu.make_async_remote_copy(
            src_ref=h1.at[c + 2 * HALF],
            dst_ref=h1.at[slot],
            send_sem=hs.at[index],
            recv_sem=hr.at[index],
            device_id=(left if side == "l" else right, ri),
            device_id_type=MESH,
        )

    def halo_arrive(i, side):
        slot = i if side == "l" else i + 2 * HALF + C
        index = i if side == "l" else i + 2 * HALF
        pltpu.make_async_remote_copy(
            src_ref=h1.at[slot], dst_ref=h1.at[slot], send_sem=hs.at[index], recv_sem=hr.at[index],
            device_id=(left if side == "l" else right, ri), device_id_type=MESH,
        ).wait_recv()

    lane = lax.broadcasted_iota(jnp.int32, (F, 128), 1)

    def shifted(src, dst, sign):
        for k in range(TAPS):
            s = sign * DILATION * (k - HALF)
            rows = slice(k * F, (k + 1) * F)
            if s == 0:
                dst[rows, :] = src.astype(BF)
                continue
            r = pltpu.roll(src, (-s) % T, 1)
            dst[rows, :] = r.astype(BF)
            if s > 0:
                dst[rows, T - 128:] = jnp.where(lane < 128 - s, r[:, T - 128:], 0.0).astype(BF)
            else:
                dst[rows, :128] = jnp.where(lane >= -s, r[:, :128], 0.0).astype(BF)

    def forward(i, carry):
        c = jnp.where(lax.rem(i, 2) == 0, i // 2, C - 1 - i // 2)
        shifted(x_ref[c].astype(F32), xcol.at[c], 1)
        for n in range(0, T, 256):
            pre2 = mm(wts[...], xcol[c, :, n:n + 256])
            for m in range(0, 256, 128):
                cols = slice(n + m, n + m + 128)
                pre = pre2[:, m:m + 128] + par[0]
                s = sigmoid(pre)
                h = pre * s
                h1[c + 2 * HALF, :, cols] = h.astype(BF)
                sl1[c, :, cols] = s + h * (1.0 - s)

        @pl.when(jnp.logical_and(has_l, c < HALF))
        def _():
            halo(c, "l").start()

        @pl.when(jnp.logical_and(has_r, c >= C - HALF))
        def _():
            halo(c, "r").start()

        return carry

    lax.fori_loop(0, C, forward, 0)
    for d in range(HALF):
        @pl.when(has_l)
        def _():
            halo(HALF + d, "l").start()

        @pl.when(has_r)
        def _():
            halo(C - HALF - 1 - d, "r").start()

    def fibre_conv(first, count, lo):
        def body(n, carry):
            cols = pl.ds(pl.multiple_of(n * 256, 256), 256)
            data = h1[lo:lo + count + 2 * HALF, :, cols].reshape((count + 2 * HALF) * F, 256)
            out = mm(wfb[:count * F, :(count + 2 * HALF) * F], data)
            z2[first:first + count, :, cols] = out.reshape(count, F, 256)
            return carry

        lax.fori_loop(0, T // 256, body, 0)

    @pl.when(has_l)
    def _():
        for i in range(HALF):
            halo_arrive(HALF + i, "l")

    fibre_conv(HALF, 4, HALF)

    @pl.when(has_r)
    def _():
        for i in range(HALF):
            halo_arrive(i, "r")

    fibre_conv(HALF + 4, 4, HALF + 4)

    def add_up(c, total_):
        for n in range(0, T, 128):
            total_ = total_ + z2[HALF + c, :, n:n + 128]
        return total_

    zero = jnp.zeros((F, 128), F32)
    own_mean = jnp.sum(lax.fori_loop(0, C, add_up, zero), axis=1, keepdims=True) / float(C * T)
    own_wide = jnp.broadcast_to(own_mean, (F, 128))

    def spread_up(c, total_):
        for n in range(0, T, 128):
            d = z2[HALF + c, :, n:n + 128] - own_wide
            total_ = total_ + d * d
        return total_

    own_m2 = jnp.sum(lax.fori_loop(0, C, spread_up, zero), axis=1, keepdims=True)
    sub = lax.broadcasted_iota(jnp.int32, (8, 128), 0)

    def tile(row0, row1):
        r0 = jnp.concatenate([row0, row0], axis=1)
        r1 = jnp.concatenate([row1, row1], axis=1)
        return jnp.where(sub == 0, jnp.broadcast_to(r0, (8, 128)), jnp.where(sub == 1, jnp.broadcast_to(r1, (8, 128)), 0.0))

    def merge(buf, n, count):
        value = [buf[i] for i in range(n)]
        avg = functools.reduce(jnp.add, value) * (1.0 / n)
        m2 = functools.reduce(jnp.add, [(v - avg) * (v - avg) for v in value]) * count
        return jnp.where(sub == 1, avg * n + pltpu.roll(m2, 1, 0), avg)

    def plain(buf, n):
        return functools.reduce(jnp.add, [buf[i] for i in range(n)])

    g_f1, g_x1, g_z1 = group_f(f1s, f1r), group_x(x1s, x1r), group_z(z1s, z1r)
    sf1[fi] = tile(to_row(own_mean), to_row(own_m2))
    g_f1.spread(sf1)
    g_f1.arrive(sf1)
    sx1[xi] = merge(sf1, nf, float(C * T))
    g_x1.spread(sx1)

    @pl.when(has_l)
    def _():
        for i in range(HALF):
            halo_arrive(i, "l")
        fibre_conv(0, HALF, 0)

    g_x1.arrive(sx1)
    sz1[zi] = merge(sx1, nx, float(C * T * nf))
    g_z1.spread(sz1)

    @pl.when(has_r)
    def _():
        for i in range(HALF):
            halo_arrive(HALF + i, "r")
        fibre_conv(HALF + C, HALF, HALF + C)

    g_z1.arrive(sz1)
    stats = merge(sz1, nz, float(C * T * nf * nx))
    mean_row = stats[0:1, :F]
    rstd_row = lax.rsqrt(stats[1:2, :F] / total + EPS)
    par[1] = wide(mean_row)
    par[2] = wide(gam_ref[...] * rstd_row)
    par[3] = wide(bet_ref[...])
    par[4] = wide(wh_ref[...].astype(F32))
    par[5] = wide(rstd_row)

    bias = bh_ref[0, 0]

    def head(c, carry):
        for n in range(0, T, 128):
            cols = slice(n, n + 128)
            zc = z2[HALF + c, :, cols] - par[1]
            act = zc * par[2] + par[3]
            s = sigmoid(act)
            h = act * s
            h2 = h.astype(BF).astype(F32)
            logit = jnp.sum(h2 * par[4], axis=0, keepdims=True) + bias
            target = lab[c, :, cols]
            soft = jnp.maximum(logit, 0.0) + jnp.log1p(jnp.exp(-jnp.abs(logit)))
            accr[0:1, :] += soft - target * logit
            dlogit = sigmoid(logit) - target
            dl[c, :, cols] = dlogit
            dh2 = (dlogit * par[4]).astype(BF).astype(F32)
            dact = dh2 * (s + h * (1.0 - s))
            sl2[HALF + c, :, cols] = dact
            acc[0] += dact
            acc[1] += dact * zc
            acc[2] += dlogit * h2
        return carry

    lax.fori_loop(0, C, head, 0)

    def dl_copy(side):
        i = 0 if side == "l" else 1
        return pltpu.make_async_remote_copy(
            src_ref=dl.at[0:HALF] if side == "l" else dl.at[C - HALF:C], dst_ref=dlr if side == "l" else dll, send_sem=ds.at[i], recv_sem=dr.at[i],
            device_id=(left if side == "l" else right, ri), device_id_type=MESH,
        )

    def dl_arrive(side):
        i = 1 if side == "l" else 0
        buf = dll if side == "l" else dlr
        pltpu.make_async_remote_copy(
            src_ref=buf, dst_ref=buf, send_sem=ds.at[i], recv_sem=dr.at[i],
            device_id=(left if side == "l" else right, ri), device_id_type=MESH,
        ).wait_recv()

    @pl.when(has_l)
    def _():
        dl_copy("l").start()

    @pl.when(has_r)
    def _():
        dl_copy("r").start()

    def lanes(v):
        return jnp.sum(v, axis=1, keepdims=True)

    g_f2, g_x2, g_z2 = group_f(f2s, f2r), group_x(x2s, x2r), group_z(z2s, z2r)
    sf2[fi] = tile(to_row(lanes(acc[0])), to_row(lanes(acc[1])))
    g_f2.spread(sf2)

    def halo_dact(slot, buf, row):
        for n in range(0, T, 128):
            cols = slice(n, n + 128)
            act = (z2[slot, :, cols] - par[1]) * par[2] + par[3]
            s = sigmoid(act)
            dh2 = (buf[row, :, cols] * par[4]).astype(BF).astype(F32)
            sl2[slot, :, cols] = dh2 * (s + act * s * (1.0 - s))

    def halo_left(i, carry):
        halo_dact(i, dll, i)
        return carry

    def halo_right(i, carry):
        halo_dact(HALF + C + i, dlr, i)
        return carry

    g_f2.arrive(sf2)
    sx2[xi] = plain(sf2, nf)
    g_x2.spread(sx2)

    @pl.when(has_l)
    def _():
        dl_arrive("l")
        lax.fori_loop(0, HALF, halo_left, 0)

    g_x2.arrive(sx2)
    sz2[zi] = plain(sx2, nx)
    g_z2.spread(sz2)

    @pl.when(has_r)
    def _():
        dl_arrive("r")
        lax.fori_loop(0, HALF, halo_right, 0)

    g_z2.arrive(sz2)
    sums = plain(sz2, nz)
    rstd_row = to_row(par[5][:, 0:1])
    beta_row = sums[0:1, :F]
    gamma_row = sums[1:2, :F] * rstd_row
    gbe_ref[...] = beta_row / cells
    gga_ref[...] = gamma_row / cells
    par[6] = wide(beta_row / total)
    par[7] = wide(gamma_row * rstd_row / total)

    def slope_back(slot, carry):
        for n in range(0, T, 128):
            cols = slice(n, n + 128)
            zc = z2[slot, :, cols] - par[1]
            dz2[slot, :, cols] = (par[2] * (sl2[slot, :, cols] - par[6] - zc * par[7])).astype(BF)
        return carry

    lax.fori_loop(jnp.where(has_l, 0, HALF), jnp.where(has_r, C + 2 * HALF, C + HALF), slope_back, 0)

    for q in range(2):
        grad = lax.dot_general(
            dz2[HALF + 4 * q:HALF + 4 * q + 4].reshape(4 * F, T),
            h1[HALF + 4 * q:HALF + 4 * q + 10].reshape(10 * F, T),
            NT, preferred_element_type=F32,
        )
        for j in range(4):
            piece = grad[j * F:(j + 1) * F, j * F:(j + TAPS) * F]
            if q == 0 and j == 0:
                gt[:, :TAPS * F] = piece
            else:
                gt[:, :TAPS * F] += piece
    col = lax.broadcasted_iota(jnp.int32, (F, F), 1)

    def pack(src, dst, first, second):
        src[:, TAPS * F:] = jnp.where(col == 0, jnp.broadcast_to(first, (F, F)), jnp.where(col == 1, jnp.broadcast_to(second, (F, F)), 0.0))
        for i in range(nf):
            rows = F // nf
            dst[i] = src[i * rows:(i + 1) * rows, :]

    loss_part = jnp.sum(accr[0:1, :], axis=1, keepdims=True)
    pack(gt, ga, lanes(acc[2]), jnp.where(lax.broadcasted_iota(jnp.int32, (F, 1), 0) == 0, jnp.broadcast_to(loss_part, (F, 1)), 0.0))
    a1, a2, a3, a4 = group_f(a1s, a1r), group_x(a2s, a2r), group_z(a3s, a3r), group_f(a4s, a4r)
    b1, b2, b3, b4 = group_f(b1s, b1r), group_x(b2s, b2r), group_z(b3s, b3r), group_f(b4s, b4r)
    a1.scatter(ga, ra)
    ra[fi] = ga[fi]

    def fibre_back(q):
        def body(n, carry):
            cols = pl.ds(pl.multiple_of(n * 256, 256), 256)
            data = dz2[4 * q:4 * q + 10, :, cols].reshape(10 * F, 256)
            out = mm(wfr[...], data).reshape(4, F, 256)
            for j in range(4):
                dh = out[j].astype(BF).astype(F32)
                value = (dh * sl1[4 * q + j, :, cols]).astype(BF)
                dz1[4 * q + j, :, cols] = value
                value = value.astype(F32)
                acc[3] += value[:, :128] + value[:, 128:]
            return carry

        lax.fori_loop(0, T // 256, body, 0)

    fibre_back(0)
    a1.arrive(ra)
    xa[xi] = plain(ra, nf)
    a2.spread(xa)
    fibre_back(1)
    a2.arrive(xa)
    za[zi] = plain(xa, nx)
    a3.spread(za)

    gt[...] = jnp.zeros_like(gt)

    def time_grad(c, carry):
        gt[:, :TAPS * F] += lax.dot_general(dz1[c], xcol[c], NT, preferred_element_type=F32)
        return carry

    lax.fori_loop(0, C, time_grad, 0)
    a3.arrive(za)
    fa[fi] = plain(za, nz)
    pack(gt, gb, lanes(acc[3]), jnp.zeros((F, 1), F32))
    b1.scatter(gb, rb)
    rb[fi] = gb[fi]
    a4.spread(fa)

    def time_back(c, carry):
        shifted(dz1[c].astype(F32), dcol, -1)
        for n in range(0, T, 256):
            gr_ref[c, :, n:n + 256] = mm(wtt[...], dcol[:, n:n + 256]).astype(BF)
        return carry

    lax.fori_loop(0, 2, time_back, 0)
    b1.arrive(rb)
    xb[xi] = plain(rb, nf)
    b2.spread(xb)
    lax.fori_loop(2, 4, time_back, 0)
    b2.arrive(xb)
    zb[zi] = plain(xb, nx)
    b3.spread(zb)
    lax.fori_loop(4, 6, time_back, 0)
    b3.arrive(zb)
    fb[fi] = plain(zb, nz)
    b4.spread(fb)
    lax.fori_loop(6, C, time_back, 0)

    a4.arrive(fa)
    rows = F // nf
    for i in range(nf):
        value = fa[i] / cells
        for k in range(TAPS):
            gwf_ref[k, i * rows:(i + 1) * rows, :] = value[:, k * F:(k + 1) * F]
    tail = fa[...].reshape(F, 8 * F)[:, TAPS * F:]
    gwh_ref[...] = to_row(tail[:, 0:1] / cells)
    loss_ref[...] = tail[0:1, 1:2] / total
    b4.arrive(fb)
    for i in range(nf):
        value = fb[i] / cells
        for k in range(TAPS):
            gwt_ref[k, i * rows:(i + 1) * rows, :] = value[:, k * F:(k + 1) * F]
    tail = fb[...].reshape(F, 8 * F)[:, TAPS * F:]
    gbt_ref[...] = to_row(tail[:, 0:1] / cells)

    for group, buf in (
        (g_f1, sf1), (g_x1, sx1), (g_z1, sz1), (g_f2, sf2), (g_x2, sx2), (g_z2, sz2),
        (a1, ga), (a2, xa), (a3, za), (a4, fa), (b1, gb), (b2, xb), (b3, zb), (b4, fb),
    ):
        group.done(buf)

    @pl.when(has_l)
    def _():
        dl_copy("l").wait_send()
        for c in range(2 * HALF):
            halo(c, "l").wait_send()

    @pl.when(has_r)
    def _():
        dl_copy("r").wait_send()
        for c in range(2 * HALF):
            halo(C - 1 - c, "r").wait_send()


def local(dims, records, labels, w_time, b_time, w_fibre, gamma, beta, w_head, b_head):
    nf, nx, nz, C, T = dims
    vm = pl.BlockSpec(memory_space=pltpu.VMEM)
    S = jax.ShapeDtypeStruct
    V = pltpu.VMEM
    D = pltpu.SemaphoreType.DMA
    rows = F // nf

    def small():
        return [V((nf, 8, 128), F32), V((nx, 8, 128), F32), V((nz, 8, 128), F32)]

    def large():
        return [V((nf, rows, 512), F32), V((nf, rows, 512), F32), V((nx, rows, 512), F32),
                V((nz, rows, 512), F32), V((nf, rows, 512), F32)]

    def sems(*sizes):
        return [D((n,)) for n in sizes for _ in range(2)]

    outs = pl.pallas_call(
        functools.partial(kernel, dims),
        out_shape=(
            S((C, F, T), BF), S((TAPS, F, F), F32), S((1, F), F32), S((TAPS, F, F), F32),
            S((1, F), F32), S((1, F), F32), S((1, F), F32), S((1, 1), F32),
        ),
        in_specs=[vm] * 8 + [pl.BlockSpec(memory_space=pltpu.SMEM)],
        out_specs=[vm] * 8,
        scratch_shapes=[
            V((F, TAPS * F), BF), V((F, TAPS * F), BF), V((4 * F, 10 * F), BF), V((4 * F, 10 * F), BF),
            V((C, TAPS * F, T), BF), V((TAPS * F, T), BF), V((C + 12, F, T), BF), V((C, F, T), F32),
            V((C + 6, F, T), F32), V((C + 6, F, T), F32), V((C + 6, F, T), BF), V((C, F, T), BF),
            V((8, F, 128), F32), V((4, F, 128), F32), V((8, 128), F32),
            V((C, 1, T), F32), V((C, 1, T), F32), V((HALF, 1, T), F32), V((HALF, 1, T), F32), V((F, 512), F32),
            *small(), *small(), *large(), *large(),
            *sems(12, 2), *sems(nf, nx, nz), *sems(nf, nx, nz),
            *sems(nf, nx, nz, nf), *sems(nf, nx, nz, nf),
        ],
        compiler_params=pltpu.CompilerParams(
            collective_id=0, has_side_effects=True, vmem_limit_bytes=56 * 1024 * 1024
        ),
    )(
        records[0], labels[0], w_time, b_time.reshape(1, F), w_fibre, gamma.reshape(1, F), beta.reshape(1, F),
        w_head.reshape(1, F), b_head.reshape(1, 1),
    )
    gr, gwt, gbt, gwf, gga, gbe, gwh, loss = outs
    return gr[None], gwt, gbt[0], gwf, gga[0], gbe[0], gwh[0], loss[0, 0]


def solution(mesh):
    nf, nr = mesh.shape["fibre"], mesh.shape["record"]
    nx = 4 if nr % 4 == 0 else 1

    def run(records, *rest):
        dims = (nf, nx, nr // nx, records.shape[1] // nf, records.shape[3])
        return jax.shard_map(
            functools.partial(local, dims),
            mesh=mesh,
            in_specs=(P("record", "fibre", None, None), P("record", "fibre", None)) + (P(),) * 7,
            out_specs=(P("record", "fibre", None, None),) + (P(),) * 7,
            check_vma=False,
        )(records, *rest)

    return run
```

time: 662 us -> 91.5 us (0.14)
  blocking collectives: 322 us -> 0 us
  waiting for transfers between devices: 203 us -> 0 us
  Pallas kernels: 0 us -> 82.2 us
  matrix products: 48.5 us -> 0 us
  local copies, waits for them, and re-layouts: 35.8 us -> 6.02 us
  other arithmetic: 21.1 us -> 0 us
  between operations: 16.8 us -> 3.07 us
  starting transfers between devices: 13.5 us -> 0 us
    psum x4 -> x0, blocking collectives: 301 us -> none  [the longest x1 78.8 us: local(): lax.psum(jnp.sum(second_preactivation, axis=(0, 1, 3)), ('fibre', 'record'))]
    psum x1 -> x0, waiting for transfers between devices: 164 us -> none  [local(): lax.psum((local_terms[0], local_terms[1], local_terms[2], local_terms[3])...]
    pallas_call x0 -> x1, Pallas kernels: none -> 82.2 us  [local(): pl.pallas_call(functools.partial(kernel, dims), out_shape=(S((C, F, T), B...]
    dot_general x44 -> x0, matrix products: 48.5 us -> none  [the longest x7 19.1 us: local(): jnp.einsum('gf,rcgs->rcfs', w_time[tap_index], dz1_pad[:, :, :, window_st...]
    all_to_all x3 -> x0, waiting for transfers between devices: 38.9 us -> none  [the longest x1 14.4 us: local(): lax.all_to_all(normed, 'fibre', split_axis=1, concat_axis=3, tiled=True)]
    all_to_all x1 -> x0, blocking collectives: 20.8 us -> none  [local(): lax.all_to_all(hidden, 'fibre', split_axis=3, concat_axis=1, tiled=True)]
    all_to_all x3 -> x0, starting transfers between devices: 13.5 us -> none  [the longest x1 4.77 us: local(): lax.all_to_all(dhidden, 'fibre', split_axis=1, concat_axis=3, tiled=True)]
    unnamed x27 -> x19, local copies, waits for them, and re-layouts: 18 us -> 6.02 us
  transfers between devices with their start and end apart: 4 -> 0, of which waited for: 4 -> 0; matrix products, arithmetic and copies ran while one was open for 2% -> 0% of each run, Pallas kernels for 0% -> 0%
where the time goes in v1:
time: 91.5 us; the launch traced here: 91.3 us
  Pallas kernels  82.2 us (90%)
  local copies, waits for them, and re-layouts  6.02 us (7%)
  between operations  3.07 us (3%)
    pallas_call x1, Pallas kernels, local(): pl.pallas_call(functools.partial(kernel, dims), out_shape=(S((C, F, T), B...  82.2 us
    unnamed x19, local copies, waits for them, and re-layouts  6.02 us

profile of v1, /device:TPU:1, one launch (start us, length us, event | category | flops | bytes accessed | tf_op | source)
XLA Modules:
  0.0 91.3 jit_solution(3533152801489274593)
XLA Ops:
  1.3 82.2 %shard_map.152 = (bf16[8,64,1024]{2,1,0:T(8,128)(2,1)}, f32[7,64,64]{2,1,0:T(8,128)}, f32[1,64]{1,0:T(1,128)}, f32[7,64,64]{2,1,0:T(8,128)}, f32[1,64]{1,0:T(1,1...) custom-call(bf16[8,64,1024]{2,1,0:T(8,128)(2,1)} %bitcast.14, s32[8,1024]{1,0:T(8,128)} %bitcast.16, ...), custom_call_target="tpu_custom_call" | custom-call | tf_op jit(solution)/shard_map/pallas_call | solution.py:564
  83.5 0.0 copy-start.1
  83.5 2.3 %copy.26 = bf16[1,8,64,1024]{3,2,1,0:T(8,128)(2,1)} copy(bf16[1,8,64,1024]{3,2,1,0:T(8,128)(2,1)} %bitcast.15) | data formatting | bytes 2097152
  85.8 0.0 copy-done.1
  85.8 0.0 copy-start.5
  85.8 0.0 copy-start
  85.8 0.7 copy.27
  86.5 0.0 copy-done.5
  86.5 0.5 copy.28
  87.0 0.0 copy-done
  87.0 0.0 copy-start.4
  87.0 0.7 copy.29
  87.7 0.0 copy-done.4
  87.7 0.0 copy-start.3
  87.7 0.5 copy.30
  88.2 0.2 copy-done.3
  88.4 0.0 copy-start.2
  88.4 0.5 copy.31
  88.9 0.1 copy-done.2
  89.0 0.5 copy.32
Async XLA Ops:
  83.5 2.3 %copy-start.1 = (f32[7,64,64]{2,1,0:T(8,128)S(1)}, f32[7,64,64]{2,1,0:T(8,128)}, u32[]{:S(2)}) copy-start(f32[7,64,64]{2,1,0:T(8,128)} %get-tuple-element.33) | copy-start | bytes 344068
  85.8 0.7 copy-start.5
  85.8 1.2 %copy-start = (f32[7,64,64]{2,1,0:T(8,128)S(1)}, f32[7,64,64]{2,1,0:T(8,128)}, u32[]{:S(2)}) copy-start(f32[7,64,64]{2,1,0:T(8,128)} %get-tuple-element.35) | copy-start | bytes 344068
  87.0 0.7 copy-start.4
  87.7 0.7 copy-start.3
  88.4 0.6 copy-start.2

commit v2 on v1

--- a/solution.py
+++ b/solution.py
@@ -23,7 +23,7 @@
 
 
 def sigmoid(v):
-    return 1.0 / (1.0 + jnp.exp(-v))
+    return 0.5 * jnp.tanh(0.5 * v) + 0.5
 
 
 def eye():
@@ -49,45 +49,42 @@
     def peers(self):
         return [lax.rem(self.me + d, self.n) for d in range(1, self.n)]
 
-    def copy(self, src, dst, p, slot):
+    def copy(self, src, dst, p):
         return pltpu.make_async_remote_copy(
-            src_ref=src,
-            dst_ref=dst,
-            send_sem=self.send.at[p],
-            recv_sem=self.recv.at[slot],
-            device_id=self.target(p),
-            device_id_type=MESH,
+            src_ref=src, dst_ref=dst, send_sem=self.send, recv_sem=self.recv,
+            device_id=self.target(p), device_id_type=MESH,
         )
 
     def spread(self, buf):
         for p in self.peers():
-            self.copy(buf.at[self.me], buf.at[self.me], p, self.me).start()
+            self.copy(buf.at[self.me], buf.at[self.me], p).start()
 
     def scatter(self, src, buf):
         for p in self.peers():
-            self.copy(src.at[p], buf.at[self.me], p, self.me).start()
+            self.copy(src.at[p], buf.at[self.me], p).start()
+
+    def all_bytes(self, buf):
+        rest = buf.at[pl.ds(0, self.n - 1)]
+        return self.copy(rest, rest, self.me)
 
     def arrive(self, buf):
-        for p in self.peers():
-            self.copy(buf.at[p], buf.at[p], p, p).wait_recv()
+        if self.n > 1:
+            self.all_bytes(buf).wait_recv()
 
     def done(self, buf):
-        for p in self.peers():
-            self.copy(buf.at[p], buf.at[p], p, p).wait_send()
+        if self.n > 1:
+            self.all_bytes(buf).wait_send()
 
 
 def kernel(
     dims,
     x_ref, lab_ref, wt_ref, bt_ref, wf_ref, gam_ref, bet_ref, wh_ref, bh_ref,
-    gr_ref, gwt_ref, gbt_ref, gwf_ref, gga_ref, gbe_ref, gwh_ref, loss_ref,
+    gr_ref, gwt_ref, gwf_ref, vec_ref,
     wts, wtt, wfb, wfr, xcol, dcol, h1, sl1, z2, sl2, dz2, dz1, par, acc, accr, lab, dl, dll, dlr,
-    gt,
-    sf1, sx1, sz1, sf2, sx2, sz2,
-    ga, ra, xa, za, fa, gb, rb, xb, zb, fb,
-    hs, hr, ds, dr,
-    f1s, f1r, x1s, x1r, z1s, z1r, f2s, f2r, x2s, x2r, z2s, z2r,
-    a1s, a1r, a2s, a2r, a3s, a3r, a4s, a4r,
-    b1s, b1r, b2s, b2r, b3s, b3r, b4s, b4r,
+    gt, gt2,
+    sp1, sz1, sp2, sz2,
+    ga, ra, za, fa, gb, rb, zb, fb,
+    hs, hr, ds, dr, sem,
 ):
     nf, nx, nz, C, T = dims
     total = float(nf * nx * nz * C * T)
@@ -96,26 +93,16 @@
     ri = lax.axis_index("record")
     xi, zi = ri // nz, lax.rem(ri, nz)
 
-    def to_f(p):
-        return (p, ri)
-
-    def to_x(p):
-        return (fi, p * nz + zi)
-
-    def to_z(p):
-        return (fi, xi * nz + p)
-
-    def group_f(s, r):
-        return Group(nf, fi, to_f, s, r)
-
-    def group_x(s, r):
-        return Group(nx, xi, to_x, s, r)
-
-    def group_z(s, r):
-        return Group(nz, zi, to_z, s, r)
+    def plane(i):
+        return Group(
+            nf * nx, fi * nx + xi, lambda p: (p // nx, lax.rem(p, nx) * nz + zi), sem.at[2 * i], sem.at[2 * i + 1]
+        )
+
+    def line(i):
+        return Group(nz, zi, lambda p: (fi, xi * nz + p), sem.at[2 * i], sem.at[2 * i + 1])
 
     barrier = pltpu.get_barrier_semaphore()
-    for group in (group_f(None, None), group_x(None, None), group_z(None, None)):
+    for group in (plane(0), line(1)):
         for p in group.peers():
             pl.semaphore_signal(barrier, inc=1, device_id=group.target(p), device_id_type=MESH)
 
@@ -136,8 +123,6 @@
     acc[...] = jnp.zeros_like(acc)
     accr[...] = jnp.zeros_like(accr)
 
-    pl.semaphore_wait(barrier, nf + nx + nz - 3)
-
     has_l, has_r = fi > 0, fi < nf - 1
     left, right = lax.rem(fi + nf - 1, nf), lax.rem(fi + 1, nf)
 
@@ -187,13 +172,13 @@
             r = pltpu.roll(src, (-s) % T, 1)
             dst[rows, :] = r.astype(BF)
             if s > 0:
-                dst[rows, T - 128:] = jnp.where(lane < 128 - s, r[:, T - 128:], 0.0).astype(BF)
+                dst[rows, T - 128:] = jnp.where(lane < 128 - s, r[:, T - 128:], jnp.zeros((), r.dtype)).astype(BF)
             else:
-                dst[rows, :128] = jnp.where(lane >= -s, r[:, :128], 0.0).astype(BF)
+                dst[rows, :128] = jnp.where(lane >= -s, r[:, :128], jnp.zeros((), r.dtype)).astype(BF)
 
     def forward(i, carry):
         c = jnp.where(lax.rem(i, 2) == 0, i // 2, C - 1 - i // 2)
-        shifted(x_ref[c].astype(F32), xcol.at[c], 1)
+        shifted(x_ref[c], xcol.at[c], 1)
         for n in range(0, T, 256):
             pre2 = mm(wts[...], xcol[c, :, n:n + 256])
             for m in range(0, 256, 128):
@@ -204,6 +189,12 @@
                 h1[c + 2 * HALF, :, cols] = h.astype(BF)
                 sl1[c, :, cols] = s + h * (1.0 - s)
 
+        return carry
+
+    def forward_send(i, carry):
+        c = jnp.where(lax.rem(i, 2) == 0, i // 2, C - 1 - i // 2)
+        forward(i, carry)
+
         @pl.when(jnp.logical_and(has_l, c < HALF))
         def _():
             halo(c, "l").start()
@@ -214,7 +205,18 @@
 
         return carry
 
-    lax.fori_loop(0, C, forward, 0)
+    lax.fori_loop(0, 2, forward, 0)
+    pl.semaphore_wait(barrier, nf * nx + nz - 2)
+
+    @pl.when(has_l)
+    def _():
+        halo(0, "l").start()
+
+    @pl.when(has_r)
+    def _():
+        halo(C - 1, "r").start()
+
+    lax.fori_loop(2, C, forward_send, 0)
     for d in range(HALF):
         @pl.when(has_l)
         def _():
@@ -264,28 +266,20 @@
         return total_
 
     own_m2 = jnp.sum(lax.fori_loop(0, C, spread_up, zero), axis=1, keepdims=True)
-    sub = lax.broadcasted_iota(jnp.int32, (8, 128), 0)
-
-    def tile(row0, row1):
-        r0 = jnp.concatenate([row0, row0], axis=1)
-        r1 = jnp.concatenate([row1, row1], axis=1)
-        return jnp.where(sub == 0, jnp.broadcast_to(r0, (8, 128)), jnp.where(sub == 1, jnp.broadcast_to(r1, (8, 128)), 0.0))
 
     def merge(buf, n, count):
-        value = [buf[i] for i in range(n)]
-        avg = functools.reduce(jnp.add, value) * (1.0 / n)
-        m2 = functools.reduce(jnp.add, [(v - avg) * (v - avg) for v in value]) * count
-        return jnp.where(sub == 1, avg * n + pltpu.roll(m2, 1, 0), avg)
-
-    def plain(buf, n):
-        return functools.reduce(jnp.add, [buf[i] for i in range(n)])
-
-    g_f1, g_x1, g_z1 = group_f(f1s, f1r), group_x(x1s, x1r), group_z(z1s, z1r)
-    sf1[fi] = tile(to_row(own_mean), to_row(own_m2))
-    g_f1.spread(sf1)
-    g_f1.arrive(sf1)
-    sx1[xi] = merge(sf1, nf, float(C * T))
-    g_x1.spread(sx1)
+        value = buf[...]
+        total_ = jnp.sum(value, axis=0)
+        d = value - total_[None] * (1.0 / n)
+        m2 = jnp.sum(d * d, axis=0) * count
+        return jnp.concatenate([total_[:, :F] * (1.0 / n), total_[:, F:] + m2[:, :F]], axis=1)
+
+    def plain(buf):
+        return jnp.sum(buf[...], axis=0)
+
+    p1, z1 = plane(0), line(1)
+    sp1[p1.me] = jnp.concatenate([to_row(own_mean), to_row(own_m2)], axis=1)
+    p1.spread(sp1)
 
     @pl.when(has_l)
     def _():
@@ -293,9 +287,9 @@
             halo_arrive(i, "l")
         fibre_conv(0, HALF, 0)
 
-    g_x1.arrive(sx1)
-    sz1[zi] = merge(sx1, nx, float(C * T * nf))
-    g_z1.spread(sz1)
+    p1.arrive(sp1)
+    sz1[zi] = merge(sp1, nf * nx, float(C * T))
+    z1.spread(sz1)
 
     @pl.when(has_r)
     def _():
@@ -303,10 +297,10 @@
             halo_arrive(HALF + i, "r")
         fibre_conv(HALF + C, HALF, HALF + C)
 
-    g_z1.arrive(sz1)
+    z1.arrive(sz1)
     stats = merge(sz1, nz, float(C * T * nf * nx))
-    mean_row = stats[0:1, :F]
-    rstd_row = lax.rsqrt(stats[1:2, :F] / total + EPS)
+    mean_row = stats[:, :F]
+    rstd_row = lax.rsqrt(stats[:, F:] / total + EPS)
     par[1] = wide(mean_row)
     par[2] = wide(gam_ref[...] * rstd_row)
     par[3] = wide(bet_ref[...])
@@ -365,9 +359,9 @@
     def lanes(v):
         return jnp.sum(v, axis=1, keepdims=True)
 
-    g_f2, g_x2, g_z2 = group_f(f2s, f2r), group_x(x2s, x2r), group_z(z2s, z2r)
-    sf2[fi] = tile(to_row(lanes(acc[0])), to_row(lanes(acc[1])))
-    g_f2.spread(sf2)
+    p2, z2_ = plane(2), line(3)
+    sp2[p2.me] = jnp.concatenate([to_row(lanes(acc[0])), to_row(lanes(acc[1]))], axis=1)
+    p2.spread(sp2)
 
     def halo_dact(slot, buf, row):
         for n in range(0, T, 128):
@@ -385,31 +379,27 @@
         halo_dact(HALF + C + i, dlr, i)
         return carry
 
-    g_f2.arrive(sf2)
-    sx2[xi] = plain(sf2, nf)
-    g_x2.spread(sx2)
-
     @pl.when(has_l)
     def _():
         dl_arrive("l")
         lax.fori_loop(0, HALF, halo_left, 0)
 
-    g_x2.arrive(sx2)
-    sz2[zi] = plain(sx2, nx)
-    g_z2.spread(sz2)
+    p2.arrive(sp2)
+    sz2[zi] = plain(sp2)
+    z2_.spread(sz2)
 
     @pl.when(has_r)
     def _():
         dl_arrive("r")
         lax.fori_loop(0, HALF, halo_right, 0)
 
-    g_z2.arrive(sz2)
-    sums = plain(sz2, nz)
+    z2_.arrive(sz2)
+    sums = plain(sz2)
     rstd_row = to_row(par[5][:, 0:1])
-    beta_row = sums[0:1, :F]
-    gamma_row = sums[1:2, :F] * rstd_row
-    gbe_ref[...] = beta_row / cells
-    gga_ref[...] = gamma_row / cells
+    beta_row = sums[:, :F]
+    gamma_row = sums[:, F:] * rstd_row
+    vec_ref[2:3, :F] = beta_row / cells
+    vec_ref[1:2, :F] = gamma_row / cells
     par[6] = wide(beta_row / total)
     par[7] = wide(gamma_row * rstd_row / total)
 
@@ -436,18 +426,20 @@
                 gt[:, :TAPS * F] += piece
     col = lax.broadcasted_iota(jnp.int32, (F, F), 1)
 
+    rows, width = F // nf, 512 // nx
+
     def pack(src, dst, first, second):
         src[:, TAPS * F:] = jnp.where(col == 0, jnp.broadcast_to(first, (F, F)), jnp.where(col == 1, jnp.broadcast_to(second, (F, F)), 0.0))
-        for i in range(nf):
-            rows = F // nf
-            dst[i] = src[i * rows:(i + 1) * rows, :]
+        for p in range(nf):
+            for q in range(nx):
+                dst[p * nx + q] = src[p * rows:(p + 1) * rows, q * width:(q + 1) * width]
 
     loss_part = jnp.sum(accr[0:1, :], axis=1, keepdims=True)
     pack(gt, ga, lanes(acc[2]), jnp.where(lax.broadcasted_iota(jnp.int32, (F, 1), 0) == 0, jnp.broadcast_to(loss_part, (F, 1)), 0.0))
-    a1, a2, a3, a4 = group_f(a1s, a1r), group_x(a2s, a2r), group_z(a3s, a3r), group_f(a4s, a4r)
-    b1, b2, b3, b4 = group_f(b1s, b1r), group_x(b2s, b2r), group_z(b3s, b3r), group_f(b4s, b4r)
+    a1, a2, a3 = plane(4), line(5), plane(6)
+    b1, b2, b3 = plane(7), line(8), plane(9)
     a1.scatter(ga, ra)
-    ra[fi] = ga[fi]
+    ra[a1.me] = ga[a1.me]
 
     def fibre_back(q):
         def body(n, carry):
@@ -465,68 +457,60 @@
         lax.fori_loop(0, T // 256, body, 0)
 
     fibre_back(0)
+    fibre_back(1)
     a1.arrive(ra)
-    xa[xi] = plain(ra, nf)
-    a2.spread(xa)
-    fibre_back(1)
-    a2.arrive(xa)
-    za[zi] = plain(xa, nx)
-    a3.spread(za)
-
-    gt[...] = jnp.zeros_like(gt)
+    za[zi] = plain(ra)
+    a2.spread(za)
+    gt2[...] = jnp.zeros_like(gt2)
 
     def time_grad(c, carry):
-        gt[:, :TAPS * F] += lax.dot_general(dz1[c], xcol[c], NT, preferred_element_type=F32)
+        gt2[...] += lax.dot_general(xcol[c], dz1[c], NT, preferred_element_type=F32)
         return carry
 
     lax.fori_loop(0, C, time_grad, 0)
-    a3.arrive(za)
-    fa[fi] = plain(za, nz)
+    for k in range(TAPS):
+        gt[:, k * F:(k + 1) * F] = gt2[k * F:(k + 1) * F, :].T
     pack(gt, gb, lanes(acc[3]), jnp.zeros((F, 1), F32))
     b1.scatter(gb, rb)
-    rb[fi] = gb[fi]
-    a4.spread(fa)
-
+    rb[b1.me] = gb[b1.me]
+    a2.arrive(za)
+    fa[a3.me] = plain(za)
+    a3.spread(fa)
     def time_back(c, carry):
-        shifted(dz1[c].astype(F32), dcol, -1)
+        shifted(dz1[c], dcol, -1)
         for n in range(0, T, 256):
             gr_ref[c, :, n:n + 256] = mm(wtt[...], dcol[:, n:n + 256]).astype(BF)
         return carry
 
-    lax.fori_loop(0, 2, time_back, 0)
+    lax.fori_loop(0, 4, time_back, 0)
     b1.arrive(rb)
-    xb[xi] = plain(rb, nf)
-    b2.spread(xb)
-    lax.fori_loop(2, 4, time_back, 0)
-    b2.arrive(xb)
-    zb[zi] = plain(xb, nx)
-    b3.spread(zb)
-    lax.fori_loop(4, 6, time_back, 0)
-    b3.arrive(zb)
-    fb[fi] = plain(zb, nz)
-    b4.spread(fb)
-    lax.fori_loop(6, C, time_back, 0)
-
-    a4.arrive(fa)
-    rows = F // nf
-    for i in range(nf):
-        value = fa[i] / cells
+    zb[zi] = plain(rb)
+    b2.spread(zb)
+    lax.fori_loop(4, C, time_back, 0)
+    b2.arrive(zb)
+    fb[b3.me] = plain(zb)
+    b3.spread(fb)
+
+    def unpack(buf, out):
+        whole = jnp.concatenate(
+            [jnp.concatenate([buf[p * nx + q] for q in range(nx)], axis=1) for p in range(nf)], axis=0
+        )
+        value = whole / cells
         for k in range(TAPS):
-            gwf_ref[k, i * rows:(i + 1) * rows, :] = value[:, k * F:(k + 1) * F]
-    tail = fa[...].reshape(F, 8 * F)[:, TAPS * F:]
-    gwh_ref[...] = to_row(tail[:, 0:1] / cells)
-    loss_ref[...] = tail[0:1, 1:2] / total
-    b4.arrive(fb)
-    for i in range(nf):
-        value = fb[i] / cells
-        for k in range(TAPS):
-            gwt_ref[k, i * rows:(i + 1) * rows, :] = value[:, k * F:(k + 1) * F]
-    tail = fb[...].reshape(F, 8 * F)[:, TAPS * F:]
-    gbt_ref[...] = to_row(tail[:, 0:1] / cells)
+            out[k] = value[:, k * F:(k + 1) * F]
+        return whole[:, TAPS * F:]
+
+    a3.arrive(fa)
+    tail = unpack(fa, gwf_ref)
+    vec_ref[3:4, :F] = to_row(tail[:, 0:1] / cells)
+    vec_ref[4:5, :F] = jnp.broadcast_to(tail[0:1, 1:2] / total, (1, F))
+    b3.arrive(fb)
+    tail = unpack(fb, gwt_ref)
+    vec_ref[0:1, :F] = to_row(tail[:, 0:1] / cells)
 
     for group, buf in (
-        (g_f1, sf1), (g_x1, sx1), (g_z1, sz1), (g_f2, sf2), (g_x2, sx2), (g_z2, sz2),
-        (a1, ga), (a2, xa), (a3, za), (a4, fa), (b1, gb), (b2, xb), (b3, zb), (b4, fb),
+        (p1, sp1), (z1, sz1), (p2, sp2), (z2_, sz2),
+        (a1, ga), (a2, za), (a3, fa), (b1, gb), (b2, zb), (b3, fb),
     ):
         group.done(buf)
 
@@ -543,41 +527,48 @@
             halo(C - 1 - c, "r").wait_send()
 
 
+def hand_out(gr, gwt, gwf, vec, gr_ref, gwt_ref, gbt_ref, gwf_ref, gga_ref, gbe_ref, gwh_ref, loss_ref, sem):
+    copies = [
+        pltpu.make_async_copy(a, b, sem.at[i])
+        for i, (a, b) in enumerate(((gr, gr_ref), (gwt, gwt_ref), (gwf, gwf_ref)))
+    ]
+    for copy in copies:
+        copy.start()
+    for i, ref in enumerate((gbt_ref, gga_ref, gbe_ref, gwh_ref)):
+        ref[...] = vec[i:i + 1, :F]
+    loss_ref[...] = vec[4:5, 0:1]
+    for copy in copies:
+        copy.wait()
+
+
 def local(dims, records, labels, w_time, b_time, w_fibre, gamma, beta, w_head, b_head):
     nf, nx, nz, C, T = dims
     vm = pl.BlockSpec(memory_space=pltpu.VMEM)
+    anywhere = pl.BlockSpec(memory_space=pl.ANY)
     S = jax.ShapeDtypeStruct
     V = pltpu.VMEM
     D = pltpu.SemaphoreType.DMA
-    rows = F // nf
-
-    def small():
-        return [V((nf, 8, 128), F32), V((nx, 8, 128), F32), V((nz, 8, 128), F32)]
+    n = nf * nx
+    rows, width = F // nf, 512 // nx
 
     def large():
-        return [V((nf, rows, 512), F32), V((nf, rows, 512), F32), V((nx, rows, 512), F32),
-                V((nz, rows, 512), F32), V((nf, rows, 512), F32)]
-
-    def sems(*sizes):
-        return [D((n,)) for n in sizes for _ in range(2)]
-
-    outs = pl.pallas_call(
+        return [V((n, rows, width), F32), V((n, rows, width), F32), V((nz, rows, width), F32), V((n, rows, width), F32)]
+
+    gr, gwt, gwf, vec = pl.pallas_call(
         functools.partial(kernel, dims),
-        out_shape=(
-            S((C, F, T), BF), S((TAPS, F, F), F32), S((1, F), F32), S((TAPS, F, F), F32),
-            S((1, F), F32), S((1, F), F32), S((1, F), F32), S((1, 1), F32),
-        ),
+        out_shape=(S((C, F, T), BF), S((TAPS, F, F), F32), S((TAPS, F, F), F32), S((8, 128), F32)),
         in_specs=[vm] * 8 + [pl.BlockSpec(memory_space=pltpu.SMEM)],
-        out_specs=[vm] * 8,
+        out_specs=[vm] * 4,
         scratch_shapes=[
             V((F, TAPS * F), BF), V((F, TAPS * F), BF), V((4 * F, 10 * F), BF), V((4 * F, 10 * F), BF),
             V((C, TAPS * F, T), BF), V((TAPS * F, T), BF), V((C + 12, F, T), BF), V((C, F, T), F32),
             V((C + 6, F, T), F32), V((C + 6, F, T), F32), V((C + 6, F, T), BF), V((C, F, T), BF),
             V((8, F, 128), F32), V((4, F, 128), F32), V((8, 128), F32),
-            V((C, 1, T), F32), V((C, 1, T), F32), V((HALF, 1, T), F32), V((HALF, 1, T), F32), V((F, 512), F32),
-            *small(), *small(), *large(), *large(),
-            *sems(12, 2), *sems(nf, nx, nz), *sems(nf, nx, nz),
-            *sems(nf, nx, nz, nf), *sems(nf, nx, nz, nf),
+            V((C, 1, T), F32), V((C, 1, T), F32), V((HALF, 1, T), F32), V((HALF, 1, T), F32),
+            V((F, 512), F32), V((TAPS * F, F), F32),
+            V((n, 1, 128), F32), V((nz, 1, 128), F32), V((n, 1, 128), F32), V((nz, 1, 128), F32),
+            *large(), *large(),
+            D((12,)), D((12,)), D((2,)), D((2,)), D((20,)),
         ],
         compiler_params=pltpu.CompilerParams(
             collective_id=0, has_side_effects=True, vmem_limit_bytes=56 * 1024 * 1024
@@ -586,7 +577,15 @@
         records[0], labels[0], w_time, b_time.reshape(1, F), w_fibre, gamma.reshape(1, F), beta.reshape(1, F),
         w_head.reshape(1, F), b_head.reshape(1, 1),
     )
-    gr, gwt, gbt, gwf, gga, gbe, gwh, loss = outs
+    row = S((1, F), F32)
+    gr, gwt, gbt, gwf, gga, gbe, gwh, loss = pl.pallas_call(
+        hand_out,
+        out_shape=(S((C, F, T), BF), S((TAPS, F, F), F32), row, S((TAPS, F, F), F32), row, row, row, S((1, 1), F32)),
+        in_specs=[vm] * 4,
+        out_specs=[anywhere, anywhere, vm, anywhere] + [vm] * 4,
+        scratch_shapes=[D((3,))],
+        compiler_params=pltpu.CompilerParams(vmem_limit_bytes=60 * 1024 * 1024),
+    )(gr, gwt, gwf, vec)
     return gr[None], gwt, gbt[0], gwf, gga[0], gbe[0], gwh[0], loss[0, 0]
 
 

time: 91.5 us -> 73.8 us (0.81)
  Pallas kernels: 82.2 us -> 72.4 us
  local copies, waits for them, and re-layouts: 6.02 us -> 0 us
  between operations: 3.07 us -> 1.29 us
    pallas_call x1, Pallas kernels: 82.2 us -> 69.4 us  [local(): pl.pallas_call(functools.partial(kernel, dims), out_shape=(S((C, F, T), B...]
    unnamed x19 -> x0, local copies, waits for them, and re-layouts: 6.02 us -> none
    pallas_call x0 -> x1, Pallas kernels: none -> 3.04 us  [local(): pl.pallas_call(hand_out, out_shape=(S((C, F, T), BF), S((TAPS, F, F), F32...]
where the time goes in v2:
time: 73.8 us; the launch traced here: 73.7 us
  Pallas kernels  72.4 us (98%)
  between operations  1.29 us (2%)
    pallas_call x1, Pallas kernels, local(): pl.pallas_call(functools.partial(kernel, dims), out_shape=(S((C, F, T), B...  69.4 us
    pallas_call x1, Pallas kernels, local(): pl.pallas_call(hand_out, out_shape=(S((C, F, T), BF), S((TAPS, F, F), F32...  3.04 us

profile of v2, /device:TPU:1, one launch (start us, length us, event | category | flops | bytes accessed | tf_op | source)
XLA Modules:
  0.0 73.7 jit_solution(14660411531603669926)
XLA Ops:
  1.3 69.4 %shard_map.152 = (bf16[8,64,1024]{2,1,0:T(8,128)(2,1)}, f32[7,64,64]{2,1,0:T(8,128)}, f32[7,64,64]{2,1,0:T(8,128)}, f32[8,128]{1,0:T(8,128)}) custom-call(bf16[8,64,1024]{2,1,0:T(8,128)(2,1)} %bitcast.14, s32[8,1024]{1,0:T(8,128)} %bitcast.15, bf16[7,64,64]{2,1,0:T(8,128)(2,1)} %wt_ref.1, f32[1,64]{1,0:T(1,128)} %bitcast.16, bf16[7,64,64]{2,1,0:T(8,128)(2,1)} %wf_ref.1, ...), custom_call_target="tpu_custom_call" | custom-call | tf_op jit(solution)/shard_map/pallas_call | solution.py:557
  70.6 3.0 %shard_map.153 = (bf16[8,64,1024]{2,1,0:T(8,128)(2,1)}, f32[7,64,64]{2,1,0:T(8,128)}, f32[1,64]{1,0:T(1,128)}, f32[7,64,64]{2,1,0:T(8,128)}, f32[1,64]{1,0:T(1,1...) custom-call(bf16[8,64,1024]{2,1,0:T(8,128)(2,1)} %get-tuple-element.20.gr, ...), custom_call_target="tpu_custom_call" | custom-call | tf_op jit(solution)/shard_map/pallas_call | solution.py:581

commit v3 on v2

--- a/solution.py
+++ b/solution.py
@@ -205,7 +205,7 @@
 
         return carry
 
-    lax.fori_loop(0, 2, forward, 0)
+    lax.fori_loop(0, 2, forward, 0, unroll=2)
     pl.semaphore_wait(barrier, nf * nx + nz - 2)
 
     @pl.when(has_l)
@@ -216,7 +216,7 @@
     def _():
         halo(C - 1, "r").start()
 
-    lax.fori_loop(2, C, forward_send, 0)
+    lax.fori_loop(2, C, forward_send, 0, unroll=6)
     for d in range(HALF):
         @pl.when(has_l)
         def _():
@@ -234,7 +234,7 @@
             z2[first:first + count, :, cols] = out.reshape(count, F, 256)
             return carry
 
-        lax.fori_loop(0, T // 256, body, 0)
+        lax.fori_loop(0, T // 256, body, 0, unroll=4)
 
     @pl.when(has_l)
     def _():
@@ -281,15 +281,15 @@
     sp1[p1.me] = jnp.concatenate([to_row(own_mean), to_row(own_m2)], axis=1)
     p1.spread(sp1)
 
+    p1.arrive(sp1)
+    sz1[zi] = merge(sp1, nf * nx, float(C * T))
+    z1.spread(sz1)
+
     @pl.when(has_l)
     def _():
         for i in range(HALF):
             halo_arrive(i, "l")
         fibre_conv(0, HALF, 0)
-
-    p1.arrive(sp1)
-    sz1[zi] = merge(sp1, nf * nx, float(C * T))
-    z1.spread(sz1)
 
     @pl.when(has_r)
     def _():
@@ -331,7 +331,7 @@
             acc[2] += dlogit * h2
         return carry
 
-    lax.fori_loop(0, C, head, 0)
+    lax.fori_loop(0, C, head, 0, unroll=4)
 
     def dl_copy(side):
         i = 0 if side == "l" else 1
@@ -410,7 +410,16 @@
             dz2[slot, :, cols] = (par[2] * (sl2[slot, :, cols] - par[6] - zc * par[7])).astype(BF)
         return carry
 
-    lax.fori_loop(jnp.where(has_l, 0, HALF), jnp.where(has_r, C + 2 * HALF, C + HALF), slope_back, 0)
+    lax.fori_loop(HALF, HALF + C, slope_back, 0, unroll=2)
+
+    @pl.when(has_l)
+    def _():
+        lax.fori_loop(0, HALF, slope_back, 0)
+
+    @pl.when(has_r)
+    def _():
+        lax.fori_loop(C + HALF, C + 2 * HALF, slope_back, 0)
+
 
     for q in range(2):
         grad = lax.dot_general(
@@ -454,39 +463,39 @@
                 acc[3] += value[:, :128] + value[:, 128:]
             return carry
 
-        lax.fori_loop(0, T // 256, body, 0)
+        lax.fori_loop(0, T // 256, body, 0, unroll=4)
 
     fibre_back(0)
     fibre_back(1)
-    a1.arrive(ra)
-    za[zi] = plain(ra)
-    a2.spread(za)
     gt2[...] = jnp.zeros_like(gt2)
 
     def time_grad(c, carry):
         gt2[...] += lax.dot_general(xcol[c], dz1[c], NT, preferred_element_type=F32)
         return carry
 
-    lax.fori_loop(0, C, time_grad, 0)
+    lax.fori_loop(0, C, time_grad, 0, unroll=8)
     for k in range(TAPS):
         gt[:, k * F:(k + 1) * F] = gt2[k * F:(k + 1) * F, :].T
     pack(gt, gb, lanes(acc[3]), jnp.zeros((F, 1), F32))
     b1.scatter(gb, rb)
     rb[b1.me] = gb[b1.me]
-    a2.arrive(za)
-    fa[a3.me] = plain(za)
-    a3.spread(fa)
+    a1.arrive(ra)
+    za[zi] = plain(ra)
+    a2.spread(za)
     def time_back(c, carry):
         shifted(dz1[c], dcol, -1)
         for n in range(0, T, 256):
             gr_ref[c, :, n:n + 256] = mm(wtt[...], dcol[:, n:n + 256]).astype(BF)
         return carry
 
-    lax.fori_loop(0, 4, time_back, 0)
+    lax.fori_loop(0, 4, time_back, 0, unroll=4)
     b1.arrive(rb)
     zb[zi] = plain(rb)
     b2.spread(zb)
-    lax.fori_loop(4, C, time_back, 0)
+    a2.arrive(za)
+    fa[a3.me] = plain(za)
+    a3.spread(fa)
+    lax.fori_loop(4, C, time_back, 0, unroll=4)
     b2.arrive(zb)
     fb[b3.me] = plain(zb)
     b3.spread(fb)
@@ -527,17 +536,23 @@
             halo(C - 1 - c, "r").wait_send()
 
 
-def hand_out(gr, gwt, gwf, vec, gr_ref, gwt_ref, gbt_ref, gwf_ref, gga_ref, gbe_ref, gwh_ref, loss_ref, sem):
-    copies = [
-        pltpu.make_async_copy(a, b, sem.at[i])
-        for i, (a, b) in enumerate(((gr, gr_ref), (gwt, gwt_ref), (gwf, gwf_ref)))
-    ]
-    for copy in copies:
+def hand_out(gr, gwt, gwf, vec, gr_ref, gwt_ref, gbt_ref, gwf_ref, gga_ref, gbe_ref, gwh_ref, loss_ref, held, sem):
+    n = held.shape[0]
+    fetch = [pltpu.make_async_copy(gr.at[i], held.at[i], sem.at[i]) for i in range(n)]
+    store = [pltpu.make_async_copy(held.at[i], gr_ref.at[i], sem.at[n + i]) for i in range(n)]
+    store.append(pltpu.make_async_copy(gwt, gwt_ref, sem.at[2 * n]))
+    store.append(pltpu.make_async_copy(gwf, gwf_ref, sem.at[2 * n + 1]))
+    for copy in fetch:
+        copy.start()
+    for copy in store[n:]:
         copy.start()
     for i, ref in enumerate((gbt_ref, gga_ref, gbe_ref, gwh_ref)):
         ref[...] = vec[i:i + 1, :F]
     loss_ref[...] = vec[4:5, 0:1]
-    for copy in copies:
+    for a, b in zip(fetch, store):
+        a.wait()
+        b.start()
+    for copy in store:
         copy.wait()
 
 
@@ -581,9 +596,9 @@
     gr, gwt, gbt, gwf, gga, gbe, gwh, loss = pl.pallas_call(
         hand_out,
         out_shape=(S((C, F, T), BF), S((TAPS, F, F), F32), row, S((TAPS, F, F), F32), row, row, row, S((1, 1), F32)),
-        in_specs=[vm] * 4,
+        in_specs=[anywhere] + [vm] * 3,
         out_specs=[anywhere, anywhere, vm, anywhere] + [vm] * 4,
-        scratch_shapes=[D((3,))],
+        scratch_shapes=[V((C, F, T), BF), D((2 * C + 2,))],
         compiler_params=pltpu.CompilerParams(vmem_limit_bytes=60 * 1024 * 1024),
     )(gr, gwt, gwf, vec)
     return gr[None], gwt, gbt[0], gwf, gga[0], gbe[0], gwh[0], loss[0, 0]

time: 73.8 us -> 68.8 us (0.932)
  Pallas kernels: 72.4 us -> 67.2 us
    pallas_call x1, Pallas kernels: 69.4 us -> 63.4 us  [local(): pl.pallas_call(functools.partial(kernel, dims), out_shape=(S((C, F, T), B...]
    pallas_call x1, Pallas kernels: 3.04 us -> 3.85 us  [local(): pl.pallas_call(hand_out, out_shape=(S((C, F, T), BF), S((TAPS, F, F), F32...]
where the time goes in v3:
time: 68.8 us; the launch traced here: 68.7 us
  Pallas kernels  67.2 us (98%)
  between operations  1.45 us (2%)
    pallas_call x1, Pallas kernels, local(): pl.pallas_call(functools.partial(kernel, dims), out_shape=(S((C, F, T), B...  63.4 us
    pallas_call x1, Pallas kernels, local(): pl.pallas_call(hand_out, out_shape=(S((C, F, T), BF), S((TAPS, F, F), F32...  3.85 us

profile of v3, /device:TPU:1, one launch (start us, length us, event | category | flops | bytes accessed | tf_op | source)
XLA Modules:
  0.0 68.7 jit_solution(11244134091931978529)
XLA Ops:
  1.3 63.4 %shard_map.152 = (bf16[8,64,1024]{2,1,0:T(8,128)(2,1)}, f32[7,64,64]{2,1,0:T(8,128)}, f32[7,64,64]{2,1,0:T(8,128)}, f32[8,128]{1,0:T(8,128)}) custom-call(bf16[8,64,1024]{2,1,0:T(8,128)(2,1)} %bitcast.14, s32[8,1024]{1,0:T(8,128)} %bitcast.15, bf16[7,64,64]{2,1,0:T(8,128)(2,1)} %wt_ref.1, f32[1,64]{1,0:T(1,128)} %bitcast.16, bf16[7,64,64]{2,1,0:T(8,128)(2,1)} %wf_ref.1, ...), custom_call_target="tpu_custom_call" | custom-call | tf_op jit(solution)/shard_map/pallas_call | solution.py:572
  64.6 3.9 %shard_map.153 = (bf16[8,64,1024]{2,1,0:T(8,128)(2,1)}, f32[7,64,64]{2,1,0:T(8,128)}, f32[1,64]{1,0:T(1,128)}, f32[7,64,64]{2,1,0:T(8,128)}, f32[1,64]{1,0:T(1,1...) custom-call(bf16[8,64,1024]{2,1,0:T(8,128)(2,1)} %get-tuple-element.20.gr, ...), custom_call_target="tpu_custom_call" | custom-call | tf_op jit(solution)/shard_map/pallas_call | solution.py:596

commit v4 on v3

--- a/solution.py
+++ b/solution.py
@@ -84,7 +84,7 @@
     gt, gt2,
     sp1, sz1, sp2, sz2,
     ga, ra, za, fa, gb, rb, zb, fb,
-    hs, hr, ds, dr, sem,
+    hs, hr, ds, dr, sem, xs, gs, io,
 ):
     nf, nx, nz, C, T = dims
     total = float(nf * nx * nz * C * T)
@@ -100,6 +100,15 @@
 
     def line(i):
         return Group(nz, zi, lambda p: (fi, xi * nz + p), sem.at[2 * i], sem.at[2 * i + 1])
+
+    def fetch(c):
+        return pltpu.make_async_copy(x_ref.at[c], xs.at[c], io.at[c])
+
+    def store(c):
+        return pltpu.make_async_copy(gs.at[c], gr_ref.at[c], io.at[C + c])
+
+    for i in range(C):
+        fetch(i // 2 if i % 2 == 0 else C - 1 - i // 2).start()
 
     barrier = pltpu.get_barrier_semaphore()
     for group in (plane(0), line(1)):
@@ -178,7 +187,8 @@
 
     def forward(i, carry):
         c = jnp.where(lax.rem(i, 2) == 0, i // 2, C - 1 - i // 2)
-        shifted(x_ref[c], xcol.at[c], 1)
+        fetch(c).wait()
+        shifted(xs[c], xcol.at[c], 1)
         for n in range(0, T, 256):
             pre2 = mm(wts[...], xcol[c, :, n:n + 256])
             for m in range(0, 256, 128):
@@ -485,7 +495,8 @@
     def time_back(c, carry):
         shifted(dz1[c], dcol, -1)
         for n in range(0, T, 256):
-            gr_ref[c, :, n:n + 256] = mm(wtt[...], dcol[:, n:n + 256]).astype(BF)
+            gs[c, :, n:n + 256] = mm(wtt[...], dcol[:, n:n + 256]).astype(BF)
+        store(c).start()
         return carry
 
     lax.fori_loop(0, 4, time_back, 0, unroll=4)
@@ -517,6 +528,8 @@
     tail = unpack(fb, gwt_ref)
     vec_ref[0:1, :F] = to_row(tail[:, 0:1] / cells)
 
+    for c in range(C):
+        store(c).wait()
     for group, buf in (
         (p1, sp1), (z1, sz1), (p2, sp2), (z2_, sz2),
         (a1, ga), (a2, za), (a3, fa), (b1, gb), (b2, zb), (b3, fb),
@@ -536,23 +549,17 @@
             halo(C - 1 - c, "r").wait_send()
 
 
-def hand_out(gr, gwt, gwf, vec, gr_ref, gwt_ref, gbt_ref, gwf_ref, gga_ref, gbe_ref, gwh_ref, loss_ref, held, sem):
-    n = held.shape[0]
-    fetch = [pltpu.make_async_copy(gr.at[i], held.at[i], sem.at[i]) for i in range(n)]
-    store = [pltpu.make_async_copy(held.at[i], gr_ref.at[i], sem.at[n + i]) for i in range(n)]
-    store.append(pltpu.make_async_copy(gwt, gwt_ref, sem.at[2 * n]))
-    store.append(pltpu.make_async_copy(gwf, gwf_ref, sem.at[2 * n + 1]))
-    for copy in fetch:
-        copy.start()
-    for copy in store[n:]:
+def hand_out(gr, gwt, gwf, vec, gr_ref, gwt_ref, gbt_ref, gwf_ref, gga_ref, gbe_ref, gwh_ref, loss_ref, sem):
+    copies = [
+        pltpu.make_async_copy(a, b, sem.at[i])
+        for i, (a, b) in enumerate(((gr, gr_ref), (gwt, gwt_ref), (gwf, gwf_ref)))
+    ]
+    for copy in copies:
         copy.start()
     for i, ref in enumerate((gbt_ref, gga_ref, gbe_ref, gwh_ref)):
         ref[...] = vec[i:i + 1, :F]
     loss_ref[...] = vec[4:5, 0:1]
-    for a, b in zip(fetch, store):
-        a.wait()
-        b.start()
-    for copy in store:
+    for copy in copies:
         copy.wait()
 
 
@@ -572,8 +579,8 @@
     gr, gwt, gwf, vec = pl.pallas_call(
         functools.partial(kernel, dims),
         out_shape=(S((C, F, T), BF), S((TAPS, F, F), F32), S((TAPS, F, F), F32), S((8, 128), F32)),
-        in_specs=[vm] * 8 + [pl.BlockSpec(memory_space=pltpu.SMEM)],
-        out_specs=[vm] * 4,
+        in_specs=[anywhere] + [vm] * 7 + [pl.BlockSpec(memory_space=pltpu.SMEM)],
+        out_specs=[anywhere] + [vm] * 3,
         scratch_shapes=[
             V((F, TAPS * F), BF), V((F, TAPS * F), BF), V((4 * F, 10 * F), BF), V((4 * F, 10 * F), BF),
             V((C, TAPS * F, T), BF), V((TAPS * F, T), BF), V((C + 12, F, T), BF), V((C, F, T), F32),
@@ -584,9 +591,10 @@
             V((n, 1, 128), F32), V((nz, 1, 128), F32), V((n, 1, 128), F32), V((nz, 1, 128), F32),
             *large(), *large(),
             D((12,)), D((12,)), D((2,)), D((2,)), D((20,)),
+            V((C, F, T), BF), V((C, F, T), BF), D((2 * C,)),
         ],
         compiler_params=pltpu.CompilerParams(
-            collective_id=0, has_side_effects=True, vmem_limit_bytes=56 * 1024 * 1024
+            collective_id=0, has_side_effects=True, vmem_limit_bytes=60 * 1024 * 1024
         ),
     )(
         records[0], labels[0], w_time, b_time.reshape(1, F), w_fibre, gamma.reshape(1, F), beta.reshape(1, F),
@@ -596,9 +604,9 @@
     gr, gwt, gbt, gwf, gga, gbe, gwh, loss = pl.pallas_call(
         hand_out,
         out_shape=(S((C, F, T), BF), S((TAPS, F, F), F32), row, S((TAPS, F, F), F32), row, row, row, S((1, 1), F32)),
-        in_specs=[anywhere] + [vm] * 3,
+        in_specs=[vm] * 4,
         out_specs=[anywhere, anywhere, vm, anywhere] + [vm] * 4,
-        scratch_shapes=[V((C, F, T), BF), D((2 * C + 2,))],
+        scratch_shapes=[D((3,))],
         compiler_params=pltpu.CompilerParams(vmem_limit_bytes=60 * 1024 * 1024),
     )(gr, gwt, gwf, vec)
     return gr[None], gwt, gbt[0], gwf, gga[0], gbe[0], gwh[0], loss[0, 0]

time: 68.8 us -> 67.5 us (0.981)
  Pallas kernels: 67.2 us -> 65.9 us
    pallas_call x1, Pallas kernels: 3.85 us -> 3.04 us  [local(): pl.pallas_call(hand_out, out_shape=(S((C, F, T), BF), S((TAPS, F, F), F32...]
where the time goes in v4:
time: 67.5 us; the launch traced here: 67.4 us
  Pallas kernels  65.9 us (98%)
  between operations  1.45 us (2%)
    pallas_call x1, Pallas kernels, local(): pl.pallas_call(functools.partial(kernel, dims), out_shape=(S((C, F, T), B...  62.9 us
    pallas_call x1, Pallas kernels, local(): pl.pallas_call(hand_out, out_shape=(S((C, F, T), BF), S((TAPS, F, F), F32...  3.04 us

profile of v4, /device:TPU:1, one launch (start us, length us, event | category | flops | bytes accessed | tf_op | source)
XLA Modules:
  0.0 67.4 jit_solution(5360754773371870639)
XLA Ops:
  1.3 62.9 %shard_map.152 = (bf16[8,64,1024]{2,1,0:T(8,128)(2,1)}, f32[7,64,64]{2,1,0:T(8,128)}, f32[7,64,64]{2,1,0:T(8,128)}, f32[8,128]{1,0:T(8,128)}) custom-call(bf16[8,64,1024]{2,1,0:T(8,128)(2,1)} %bitcast.14, s32[8,1024]{1,0:T(8,128)} %bitcast.15, bf16[7,64,64]{2,1,0:T(8,128)(2,1)} %wt_ref.1, f32[1,64]{1,0:T(1,128)} %bitcast.16, bf16[7,64,64]{2,1,0:T(8,128)(2,1)} %wf_ref.1, ...), custom_call_target="tpu_custom_call" | custom-call | tf_op jit(solution)/shard_map/pallas_call | solution.py:579
  64.2 3.0 %shard_map.153 = (bf16[8,64,1024]{2,1,0:T(8,128)(2,1)}, f32[7,64,64]{2,1,0:T(8,128)}, f32[1,64]{1,0:T(1,128)}, f32[7,64,64]{2,1,0:T(8,128)}, f32[1,64]{1,0:T(1,1...) custom-call(bf16[8,64,1024]{2,1,0:T(8,128)(2,1)} %get-tuple-element.20.gr, ...), custom_call_target="tpu_custom_call" | custom-call | tf_op jit(solution)/shard_map/pallas_call | solution.py:604

commit v5 on v4

--- a/solution.py
+++ b/solution.py
@@ -81,7 +81,7 @@
     x_ref, lab_ref, wt_ref, bt_ref, wf_ref, gam_ref, bet_ref, wh_ref, bh_ref,
     gr_ref, gwt_ref, gwf_ref, vec_ref,
     wts, wtt, wfb, wfr, xcol, dcol, h1, sl1, z2, sl2, dz2, dz1, par, acc, accr, lab, dl, dll, dlr,
-    gt, gt2,
+    gt,
     sp1, sz1, sp2, sz2,
     ga, ra, za, fa, gb, rb, zb, fb,
     hs, hr, ds, dr, sem, xs, gs, io,
@@ -117,20 +117,7 @@
 
     for k in range(TAPS):
         wts[:, k * F:(k + 1) * F] = wt_ref[k]
-        wtt[:, k * F:(k + 1) * F] = wt_ref[k].astype(F32).T.astype(BF)
-    wfb[...] = jnp.zeros_like(wfb)
-    wfr[...] = jnp.zeros_like(wfr)
-    for k in range(TAPS):
-        w = wf_ref[k]
-        wr = wf_ref[TAPS - 1 - k].astype(F32).T.astype(BF)
-        for j in range(4):
-            wfb[j * F:(j + 1) * F, (j + k) * F:(j + k + 1) * F] = w
-            wfr[j * F:(j + 1) * F, (j + k) * F:(j + k + 1) * F] = wr
-    for c in range(C):
-        lab[c] = lab_ref[c:c + 1, :].astype(F32)
     par[0] = wide(bt_ref[...])
-    acc[...] = jnp.zeros_like(acc)
-    accr[...] = jnp.zeros_like(accr)
 
     has_l, has_r = fi > 0, fi < nf - 1
     left, right = lax.rem(fi + nf - 1, nf), lax.rem(fi + 1, nf)
@@ -236,6 +223,23 @@
         def _():
             halo(C - HALF - 1 - d, "r").start()
 
+    for k in range(TAPS):
+        wtt[:, k * F:(k + 1) * F] = wt_ref[k].astype(F32).T.astype(BF)
+    wfb[...] = jnp.zeros_like(wfb)
+    wfr[...] = jnp.zeros_like(wfr)
+    for k in range(TAPS):
+        w = wf_ref[k]
+        wr = wf_ref[TAPS - 1 - k].astype(F32).T.astype(BF)
+        for j in range(4):
+            wfb[j * F:(j + 1) * F, (j + k) * F:(j + k + 1) * F] = w
+            wfr[j * F:(j + 1) * F, (j + k) * F:(j + k + 1) * F] = wr
+    for c in range(C):
+        lab[c] = lab_ref[c:c + 1, :].astype(F32)
+    par[3] = wide(bet_ref[...])
+    par[4] = wide(wh_ref[...].astype(F32))
+    acc[...] = jnp.zeros_like(acc)
+    accr[...] = jnp.zeros_like(accr)
+
     def fibre_conv(first, count, lo):
         def body(n, carry):
             cols = pl.ds(pl.multiple_of(n * 256, 256), 256)
@@ -266,7 +270,7 @@
         return total_
 
     zero = jnp.zeros((F, 128), F32)
-    own_mean = jnp.sum(lax.fori_loop(0, C, add_up, zero), axis=1, keepdims=True) / float(C * T)
+    own_mean = jnp.sum(lax.fori_loop(0, C, add_up, zero, unroll=8), axis=1, keepdims=True) / float(C * T)
     own_wide = jnp.broadcast_to(own_mean, (F, 128))
 
     def spread_up(c, total_):
@@ -275,7 +279,7 @@
             total_ = total_ + d * d
         return total_
 
-    own_m2 = jnp.sum(lax.fori_loop(0, C, spread_up, zero), axis=1, keepdims=True)
+    own_m2 = jnp.sum(lax.fori_loop(0, C, spread_up, zero, unroll=8), axis=1, keepdims=True)
 
     def merge(buf, n, count):
         value = buf[...]
@@ -313,9 +317,6 @@
     rstd_row = lax.rsqrt(stats[:, F:] / total + EPS)
     par[1] = wide(mean_row)
     par[2] = wide(gam_ref[...] * rstd_row)
-    par[3] = wide(bet_ref[...])
-    par[4] = wide(wh_ref[...].astype(F32))
-    par[5] = wide(rstd_row)
 
     bias = bh_ref[0, 0]
 
@@ -405,7 +406,6 @@
 
     z2_.arrive(sz2)
     sums = plain(sz2)
-    rstd_row = to_row(par[5][:, 0:1])
     beta_row = sums[:, :F]
     gamma_row = sums[:, F:] * rstd_row
     vec_ref[2:3, :F] = beta_row / cells
@@ -420,7 +420,7 @@
             dz2[slot, :, cols] = (par[2] * (sl2[slot, :, cols] - par[6] - zc * par[7])).astype(BF)
         return carry
 
-    lax.fori_loop(HALF, HALF + C, slope_back, 0, unroll=2)
+    lax.fori_loop(HALF, HALF + C, slope_back, 0, unroll=4)
 
     @pl.when(has_l)
     def _():
@@ -477,15 +477,13 @@
 
     fibre_back(0)
     fibre_back(1)
-    gt2[...] = jnp.zeros_like(gt2)
+    gt[...] = jnp.zeros_like(gt)
 
     def time_grad(c, carry):
-        gt2[...] += lax.dot_general(xcol[c], dz1[c], NT, preferred_element_type=F32)
+        gt[:, :TAPS * F] += lax.dot_general(dz1[c], xcol[c], NT, preferred_element_type=F32)
         return carry
 
     lax.fori_loop(0, C, time_grad, 0, unroll=8)
-    for k in range(TAPS):
-        gt[:, k * F:(k + 1) * F] = gt2[k * F:(k + 1) * F, :].T
     pack(gt, gb, lanes(acc[3]), jnp.zeros((F, 1), F32))
     b1.scatter(gb, rb)
     rb[b1.me] = gb[b1.me]
@@ -515,7 +513,7 @@
         whole = jnp.concatenate(
             [jnp.concatenate([buf[p * nx + q] for q in range(nx)], axis=1) for p in range(nf)], axis=0
         )
-        value = whole / cells
+        value = whole * (1.0 / cells)
         for k in range(TAPS):
             out[k] = value[:, k * F:(k + 1) * F]
         return whole[:, TAPS * F:]
@@ -549,17 +547,37 @@
             halo(C - 1 - c, "r").wait_send()
 
 
-def hand_out(gr, gwt, gwf, vec, gr_ref, gwt_ref, gbt_ref, gwf_ref, gga_ref, gbe_ref, gwh_ref, loss_ref, sem):
-    copies = [
-        pltpu.make_async_copy(a, b, sem.at[i])
-        for i, (a, b) in enumerate(((gr, gr_ref), (gwt, gwt_ref), (gwf, gwf_ref)))
+def hand_out(
+    gr, gwt, gwf, vec, gr_ref, gwt_ref, gbt_ref, gwf_ref, gga_ref, gbe_ref, gwh_ref, loss_ref,
+    gr_s, gwt_s, gwf_s, vec_s, gbt_s, gga_s, gbe_s, gwh_s, loss_s, come, go,
+):
+    half = gr_s.shape[0] // 2
+    first, second = pl.ds(0, half), pl.ds(half, half)
+    fetch = [
+        pltpu.make_async_copy(a, b, come.at[i])
+        for i, (a, b) in enumerate((
+            (vec, vec_s), (gr.at[first], gr_s.at[first]), (gr.at[second], gr_s.at[second]), (gwt, gwt_s), (gwf, gwf_s),
+        ))
     ]
-    for copy in copies:
+    store = [
+        pltpu.make_async_copy(a, b, go.at[i])
+        for i, (a, b) in enumerate((
+            (gr_s.at[first], gr_ref.at[first]), (gr_s.at[second], gr_ref.at[second]), (gwt_s, gwt_ref), (gwf_s, gwf_ref),
+            (gbt_s, gbt_ref), (gga_s, gga_ref), (gbe_s, gbe_ref), (gwh_s, gwh_ref), (loss_s, loss_ref),
+        ))
+    ]
+    for copy in fetch:
         copy.start()
-    for i, ref in enumerate((gbt_ref, gga_ref, gbe_ref, gwh_ref)):
-        ref[...] = vec[i:i + 1, :F]
-    loss_ref[...] = vec[4:5, 0:1]
-    for copy in copies:
+    fetch[0].wait()
+    for i, ref in enumerate((gbt_s, gga_s, gbe_s, gwh_s)):
+        ref[...] = vec_s[i:i + 1, :F]
+    loss_s[...] = vec_s[4:5, 0:1]
+    for copy in store[4:]:
+        copy.start()
+    for a, b in zip(fetch[1:], store[:4]):
+        a.wait()
+        b.start()
+    for copy in store:
         copy.wait()
 
 
@@ -587,7 +605,7 @@
             V((C + 6, F, T), F32), V((C + 6, F, T), F32), V((C + 6, F, T), BF), V((C, F, T), BF),
             V((8, F, 128), F32), V((4, F, 128), F32), V((8, 128), F32),
             V((C, 1, T), F32), V((C, 1, T), F32), V((HALF, 1, T), F32), V((HALF, 1, T), F32),
-            V((F, 512), F32), V((TAPS * F, F), F32),
+            V((F, 512), F32),
             V((n, 1, 128), F32), V((nz, 1, 128), F32), V((n, 1, 128), F32), V((nz, 1, 128), F32),
             *large(), *large(),
             D((12,)), D((12,)), D((2,)), D((2,)), D((20,)),
@@ -604,9 +622,12 @@
     gr, gwt, gbt, gwf, gga, gbe, gwh, loss = pl.pallas_call(
         hand_out,
         out_shape=(S((C, F, T), BF), S((TAPS, F, F), F32), row, S((TAPS, F, F), F32), row, row, row, S((1, 1), F32)),
-        in_specs=[vm] * 4,
-        out_specs=[anywhere, anywhere, vm, anywhere] + [vm] * 4,
-        scratch_shapes=[D((3,))],
+        in_specs=[anywhere] * 4,
+        out_specs=[anywhere] * 8,
+        scratch_shapes=[
+            V((C, F, T), BF), V((TAPS, F, F), F32), V((TAPS, F, F), F32), V((8, 128), F32),
+            V((1, F), F32), V((1, F), F32), V((1, F), F32), V((1, F), F32), V((1, 1), F32), D((5,)), D((9,)),
+        ],
         compiler_params=pltpu.CompilerParams(vmem_limit_bytes=60 * 1024 * 1024),
     )(gr, gwt, gwf, vec)
     return gr[None], gwt, gbt[0], gwf, gga[0], gbe[0], gwh[0], loss[0, 0]

time: 67.5 us -> 66.4 us (0.984)
  Pallas kernels: 65.9 us -> 64.7 us
    pallas_call x1, Pallas kernels: 3.04 us -> 2.29 us  [local(): pl.pallas_call(hand_out, out_shape=(S((C, F, T), BF), S((TAPS, F, F), F32...]
where the time goes in v5:
time: 66.4 us; the launch traced here: 66.2 us
  Pallas kernels  64.7 us (97%)
  between operations  1.45 us (2%)
    pallas_call x1, Pallas kernels, local(): pl.pallas_call(functools.partial(kernel, dims), out_shape=(S((C, F, T), B...  62.5 us
    pallas_call x1, Pallas kernels, local(): pl.pallas_call(hand_out, out_shape=(S((C, F, T), BF), S((TAPS, F, F), F32...  2.29 us

profile of v5, /device:TPU:1, one launch (start us, length us, event | category | flops | bytes accessed | tf_op | source)
XLA Modules:
  0.0 66.2 jit_solution(12785213073546377330)
XLA Ops:
  1.3 62.5 %shard_map.152 = (bf16[8,64,1024]{2,1,0:T(8,128)(2,1)}, f32[7,64,64]{2,1,0:T(8,128)}, f32[7,64,64]{2,1,0:T(8,128)}, f32[8,128]{1,0:T(8,128)}) custom-call(bf16[8,64,1024]{2,1,0:T(8,128)(2,1)} %bitcast.14, s32[8,1024]{1,0:T(8,128)} %bitcast.15, bf16[7,64,64]{2,1,0:T(8,128)(2,1)} %wt_ref.1, f32[1,64]{1,0:T(1,128)} %bitcast.16, bf16[7,64,64]{2,1,0:T(8,128)(2,1)} %wf_ref.1, ...), custom_call_target="tpu_custom_call" | custom-call | tf_op jit(solution)/shard_map/pallas_call | solution.py:597
  63.8 2.3 %shard_map.153 = (bf16[8,64,1024]{2,1,0:T(8,128)(2,1)}, f32[7,64,64]{2,1,0:T(8,128)}, f32[1,64]{1,0:T(1,128)}, f32[7,64,64]{2,1,0:T(8,128)}, f32[1,64]{1,0:T(1,1...) custom-call(bf16[8,64,1024]{2,1,0:T(8,128)(2,1)} %get-tuple-element.20.gr, ...), custom_call_target="tpu_custom_call" | custom-call | tf_op jit(solution)/shard_map/pallas_call | solution.py:622

commit v6 on v5

--- a/solution.py
+++ b/solution.py
@@ -522,15 +522,11 @@
     tail = unpack(fa, gwf_ref)
     vec_ref[3:4, :F] = to_row(tail[:, 0:1] / cells)
     vec_ref[4:5, :F] = jnp.broadcast_to(tail[0:1, 1:2] / total, (1, F))
-    b3.arrive(fb)
-    tail = unpack(fb, gwt_ref)
-    vec_ref[0:1, :F] = to_row(tail[:, 0:1] / cells)
-
     for c in range(C):
         store(c).wait()
     for group, buf in (
         (p1, sp1), (z1, sz1), (p2, sp2), (z2_, sz2),
-        (a1, ga), (a2, za), (a3, fa), (b1, gb), (b2, zb), (b3, fb),
+        (a1, ga), (a2, za), (a3, fa), (b1, gb), (b2, zb),
     ):
         group.done(buf)
 
@@ -545,6 +541,12 @@
         dl_copy("r").wait_send()
         for c in range(2 * HALF):
             halo(C - 1 - c, "r").wait_send()
+
+    b3.arrive(fb)
+    tail = unpack(fb, gwt_ref)
+    vec_ref[0:1, :F] = to_row(tail[:, 0:1] / cells)
+
+    b3.done(fb)
 
 
 def hand_out(

time: 66.4 us -> 66.3 us (level)
  no operation moved by 1% of the time
where the time goes in v6:
time: 66.3 us; the launch traced here: 66.2 us
  Pallas kernels  64.7 us (98%)
  between operations  1.45 us (2%)
    pallas_call x1, Pallas kernels, local(): pl.pallas_call(functools.partial(kernel, dims), out_shape=(S((C, F, T), B...  62.4 us
    pallas_call x1, Pallas kernels, local(): pl.pallas_call(hand_out, out_shape=(S((C, F, T), BF), S((TAPS, F, F), F32...  2.29 us

profile of v6, /device:TPU:1, one launch (start us, length us, event | category | flops | bytes accessed | tf_op | source)
XLA Modules:
  0.0 66.2 jit_solution(4309128857467573870)
XLA Ops:
  1.3 62.4 %shard_map.152 = (bf16[8,64,1024]{2,1,0:T(8,128)(2,1)}, f32[7,64,64]{2,1,0:T(8,128)}, f32[7,64,64]{2,1,0:T(8,128)}, f32[8,128]{1,0:T(8,128)}) custom-call(bf16[8,64,1024]{2,1,0:T(8,128)(2,1)} %bitcast.14, s32[8,1024]{1,0:T(8,128)} %bitcast.15, bf16[7,64,64]{2,1,0:T(8,128)(2,1)} %wt_ref.1, f32[1,64]{1,0:T(1,128)} %bitcast.16, bf16[7,64,64]{2,1,0:T(8,128)(2,1)} %wf_ref.1, ...), custom_call_target="tpu_custom_call" | custom-call | tf_op jit(solution)/shard_map/pallas_call | solution.py:599
  63.7 2.3 %shard_map.153 = (bf16[8,64,1024]{2,1,0:T(8,128)(2,1)}, f32[7,64,64]{2,1,0:T(8,128)}, f32[1,64]{1,0:T(1,128)}, f32[7,64,64]{2,1,0:T(8,128)}, f32[1,64]{1,0:T(1,1...) custom-call(bf16[8,64,1024]{2,1,0:T(8,128)(2,1)} %get-tuple-element.20.gr, ...), custom_call_target="tpu_custom_call" | custom-call | tf_op jit(solution)/shard_map/pallas_call | solution.py:624
